TPU v7x, 32 devices: a whole 2x2x4 slice. The times are simulated.
32 devices in a mesh: lat: 2 (over x), lon: 16 (over z, y, core).
Axes of the slice: x: 2, y: 2, z: 4, core: 2. Of those that a mesh axis runs over, the one named last changes fastest.
Arguments:
- tracer: float32 [4, 512, 2048], P(None, 'lat', 'lon'), may hold values from -6 to 6
- wind_east: float32 [4, 512, 2048], P(None, 'lat', 'lon'), may hold values from -4 to 4
- wind_north: float32 [4, 512, 2048], P(None, 'lat', 'lon'), may hold values from -4 to 4
- kappa: float32 [4, 512, 2048], P(None, 'lat', 'lon'), may hold values from 0.25 to 4
- cutoff: int32 [128], replicated, may hold values from 64 to 511
- partner: int32 [2048], replicated, may hold values from 0 to 2047, as said below
Outputs:
- filtered: float32 [4, 512, 2048], P(None, 'lat', 'lon')
- balanced: float32 [4, 512, 2048], P(None, 'lat', 'lon')
Inputs may be any that keep to these rules, and one draw needn't show every extreme that they name: partner[j] = (j + 1024 + s_j) mod 2048 with each column's own shift s_j of 0 to 127; some column has s_j = 127.
All inputs are finite; a program needn't handle non-finite values.
Results may differ from a plain program's by a relative error of at most 0.00005.
Values sent between devices are 32-bit elements; how exact they have to be, the bound alone decides.
A program may use at most 64 MiB of HBM per device.

v0:
```python
import functools
import math

import jax
import jax.numpy as jnp
import numpy as np
from jax import lax
from jax.experimental import pallas as pl
from jax.experimental.pallas import tpu as pltpu
from jax.sharding import PartitionSpec as P

KMAX = 512
SWEEPS = 4
COURANT = 0.4
HIGHEST = lax.Precision.HIGHEST


def tables(sectors, width):
    total = sectors * width
    half = sectors // 2
    m = np.arange(width)
    theta = 2.0 * np.pi * (np.outer(np.arange(half + 1), m) % total) / total
    kept = 2 * KMAX // sectors
    k2 = np.arange(kept) - kept // 2
    phase = 2.0 * np.pi * (np.outer(m, k2) % width) / width
    c, s = np.cos(phase), np.sin(phase)
    forward = np.block([[c, -s], [s, c]])
    inverse = np.block([[c.T, s.T], [-s.T, c.T]]) / total
    return [a.astype(np.float32) for a in (np.cos(theta), np.sin(theta), forward, inverse)]


def weighted(terms):
    total = None
    for factor, value in terms:
        if abs(factor) < 1e-12:
            continue
        part = value if abs(factor - 1.0) < 1e-12 else value * np.float32(factor)
        total = part if total is None else total + part
    return total


def taken(x, at_lane):
    return jnp.take_along_axis(x, at_lane, axis=1, mode="promise_in_bounds")


def kernel(
    sectors, bands,
    tracer_h, wind_east_h, wind_north_h, kappa_h, cutoff_h, partner_h, tw_cos_h, tw_sin_h, fwd_h, inv_h,
    filtered, balanced,
    tracer, wind_east, wind_north, kappa, cutoff, partner, tw_cos, tw_sin, fwd, inv, load_s,
    col_send, col_recv, edge_send, edge_recv, stage, spread, send_b, recv_b, coupling, scaled, ping, pong,
    halo_ss, halo_rs, a_ss, a_rs, b_ss, b_rs,
):
    lev, rows, width = tracer.shape
    pole = cutoff.shape[1] // 2
    share = lev * pole // sectors
    slices = sectors // lev
    half = sectors // 2
    groups = lev * rows // 8
    per = rows // 8
    lat = lax.axis_index("lat")
    lon = lax.axis_index("lon")

    def sector(offset):
        return lax.rem(lon + (offset % sectors), sectors)

    def band(offset):
        return lax.rem(lat + (offset % bands), bands)

    held = (tracer_h, partner_h, wind_east_h, wind_north_h, kappa_h, cutoff_h, tw_cos_h, tw_sin_h, fwd_h, inv_h)
    near = (tracer, partner, wind_east, wind_north, kappa, cutoff, tw_cos, tw_sin, fwd, inv)
    loads = [pltpu.make_async_copy(h, v, load_s.at[i]) for i, (h, v) in enumerate(zip(held, near))]
    for load in loads:
        load.start()

    barrier = pltpu.get_barrier_semaphore()
    for t in range(1, sectors):
        pl.semaphore_signal(barrier, inc=1, device_id=(lat, sector(t)), device_id_type=pl.DeviceIdType.MESH)
    beside = (1,) if bands == 2 else (1, -1)
    for t in beside:
        pl.semaphore_signal(barrier, inc=1, device_id=(band(t), lon), device_id_type=pl.DeviceIdType.MESH)
    pl.semaphore_wait(barrier, sectors - 1 + len(beside))

    loads[0].wait()
    loads[1].wait()
    lane2 = lax.broadcasted_iota(jnp.int32, (rows, width), 1)
    row2 = lax.broadcasted_iota(jnp.int32, (rows, width), 0)
    diagonal = lax.broadcasted_iota(jnp.int32, (groups, 8, width), 0) == lax.broadcasted_iota(
        jnp.int32, (groups, 8, width), 2
    )
    reach = partner[pl.ds(lon, 1), :] - sector(half) * width
    reach = jnp.where(reach < 0, reach + sectors * width, reach)
    beyond = jnp.broadcast_to(reach >= width, (2 * lev, width))
    at_lane = jnp.broadcast_to(jnp.where(reach >= width, reach - width, reach), (2 * lev, width))
    lane8 = lax.broadcasted_iota(jnp.int32, (8, width), 1)
    row8 = lax.broadcasted_iota(jnp.int32, (8, width), 0)
    inner = lax.rem(lane8, per)
    level_of = lax.broadcasted_iota(jnp.int32, (lev, width), 0) * per
    place = lax.broadcasted_iota(jnp.int32, (lev, width), 1)
    head, tail = place == level_of, place == level_of + per - 1

    def column(field, at):
        whole = field[...].reshape(groups, 8, width)
        return jnp.sum(jnp.where(diagonal, whole[:, :, at : at + 1], 0.0), axis=0)

    def border(field, depth):
        return jnp.concatenate(
            [field[l, depth : depth + 1, :] for l in range(lev)]
            + [field[l, rows - 1 - depth : rows - depth, :] for l in range(lev)],
            axis=0,
        )

    def post(turn, edge, first_column, last_column):
        edge_send[turn] = edge
        col_send[turn, 0] = last_column
        col_send[turn, 1] = first_column
        plan = [
            (edge_send.at[turn], edge_recv.at[turn, 0], (lat, sector(-half))),
            (edge_send.at[turn], edge_recv.at[turn, 1], (lat, sector(-half - 1))),
            (edge_send.at[turn], edge_recv.at[turn, 2], (band(1), lon)),
            (col_send.at[turn, 0], col_recv.at[turn, 0], (lat, sector(1))),
            (col_send.at[turn, 1], col_recv.at[turn, 1], (lat, sector(-1))),
        ]
        if bands != 2:
            plan.append((edge_send.at[turn], edge_recv.at[turn, 3], (band(-1), lon)))
        copies = []
        for i, (src, dst, device) in enumerate(plan):
            copy = pltpu.make_async_remote_copy(
                src_ref=src, dst_ref=dst, send_sem=halo_ss.at[turn, i], recv_sem=halo_rs.at[turn, i],
                device_id=device, device_id_type=pl.DeviceIdType.MESH,
            )
            copy.start()
            copies.append(copy)
        return copies

    def outer(turn):
        across = jnp.where(beyond, taken(edge_recv[turn, 1], at_lane), taken(edge_recv[turn, 0], at_lane))
        top = jnp.where(lat == 0, across[:lev], edge_recv[turn, 2, lev:])
        bottom = jnp.where(lat == bands - 1, across[lev:], edge_recv[turn, 2 if bands == 2 else 3, :lev])
        return top, bottom

    def sides(turn, top, bottom):
        west = jnp.sum(jnp.where(diagonal, col_recv[turn, 0][None], 0.0), axis=2, keepdims=True)
        east = jnp.sum(jnp.where(diagonal, col_recv[turn, 1][None], 0.0), axis=2, keepdims=True)
        return top, bottom, west, east

    def along(packed, top, bottom, at):
        above = jnp.sum(jnp.where(head, top[:, at : at + 1], 0.0), axis=0, keepdims=True)
        below = jnp.sum(jnp.where(tail, bottom[:, at : at + 1], 0.0), axis=0, keepdims=True)
        up, down = pltpu.roll(packed, 1, 0), pltpu.roll(packed, 7, 0)
        up = jnp.where(row8 == 0, jnp.where(inner == 0, above, pltpu.roll(up, 1, 1)), up)
        down = jnp.where(row8 == 7, jnp.where(inner == per - 1, below, pltpu.roll(down, width - 1, 1)), down)
        return up + down

    def ends(packed):
        return jnp.concatenate(
            [
                jnp.sum(jnp.where(head, packed[0:1], 0.0), axis=1, keepdims=True),
                jnp.sum(jnp.where(tail, packed[7:8], 0.0), axis=1, keepdims=True),
            ],
            axis=0,
        )

    def around(field, l, edges):
        top, bottom, west, east = edges
        x = field[l]
        w = jnp.broadcast_to(west[per * l : per * (l + 1)], (per, 8, width)).reshape(rows, width)
        e = jnp.broadcast_to(east[per * l : per * (l + 1)], (per, 8, width)).reshape(rows, width)
        return (
            jnp.where(lane2 == 0, w, pltpu.roll(x, 1, 1)),
            jnp.where(lane2 == width - 1, e, pltpu.roll(x, width - 1, 1)),
            jnp.where(row2 == 0, top[l : l + 1], pltpu.roll(x, 1, 0)),
            jnp.where(row2 == rows - 1, bottom[l : l + 1], pltpu.roll(x, rows - 1, 0)),
        )

    copies = post(0, border(tracer, 0), column(tracer, 0), column(tracer, width - 1))
    for load in loads[2:]:
        load.wait()
    for l in range(lev):
        inverse = 1.0 / (1.0 + 4.0 * kappa[l])
        scaled[l] = inverse
        coupling[l] = kappa[l] * inverse
    last = lat == bands - 1
    base = pl.multiple_of(jnp.where(last, rows - pole, 0), 8)
    before = jnp.where(last, rows - pole - 1, 0)
    after = jnp.where(last, rows - 1, pole)
    offset = jnp.where(last, (rows - pole) // 8, 0)
    shape = (pole // 8, 8, width)
    lane_p = lax.broadcasted_iota(jnp.int32, (pole, width), 1)
    row_p = lax.broadcasted_iota(jnp.int32, (pole, width), 0)
    for copy in copies:
        copy.wait()
    top, bottom = outer(0)

    def spoke(packed, l):
        mine = lax.broadcasted_iota(jnp.int32, shape, 0) + (per * l + offset) == lax.broadcasted_iota(
            jnp.int32, shape, 2
        )
        value = jnp.sum(jnp.where(mine, packed[None], 0.0), axis=2, keepdims=True)
        return jnp.broadcast_to(value, shape).reshape(pole, width)

    def to_share(l, q):
        device = l * slices + q
        return pltpu.make_async_remote_copy(
            src_ref=stage.at[l, pl.ds(q * share, share), :], dst_ref=spread.at[lon],
            send_sem=a_ss.at[device], recv_sem=a_rs.at[lon],
            device_id=(lat, device), device_id_type=pl.DeviceIdType.MESH,
        )

    for l in range(lev):
        x = tracer[l, pl.ds(base, pole), :]
        w = jnp.where(lane_p == 0, spoke(col_recv[0, 0], l), pltpu.roll(x, 1, 1))
        e = jnp.where(lane_p == width - 1, spoke(col_recv[0, 1], l), pltpu.roll(x, width - 1, 1))
        above = jnp.where(last, tracer[l, pl.ds(before, 1), :], top[l : l + 1])
        below = jnp.where(last, bottom[l : l + 1], tracer[l, pl.ds(after, 1), :])
        u = jnp.where(row_p == 0, above, pltpu.roll(x, 1, 0))
        d = jnp.where(row_p == pole - 1, below, pltpu.roll(x, pole - 1, 0))
        stage[l] = x - COURANT * 0.5 * (
            wind_east[l, pl.ds(base, pole), :] * (e - w) + wind_north[l, pl.ds(base, pole), :] * (d - u)
        )
        for q in range(slices):
            @pl.when(lon != l * slices + q)
            def _(l=l, q=q):
                to_share(l, q).start()

            @pl.when(lon == l * slices + q)
            def _(l=l, q=q):
                spread[l * slices + q] = stage[l, q * share : (q + 1) * share, :]

    edges = sides(0, top, bottom)
    for l in range(lev):
        w, e, u, d = around(tracer, l, edges)
        filtered[l] = tracer[l] - COURANT * 0.5 * (wind_east[l] * (e - w) + wind_north[l] * (d - u))
    fixed = [(border(a, 0), column(a, 0), column(a, width - 1)) for a in (scaled, coupling)]

    first = jnp.where(lat == bands - 1, pole, 0) + lax.rem(lon, slices) * share
    spot = lax.broadcasted_iota(jnp.int32, (share, 2 * pole), 0) + first
    limit = jnp.sum(
        jnp.where(
            lax.broadcasted_iota(jnp.int32, (share, 2 * pole), 1) == spot,
            cutoff[...].astype(jnp.float32), 0.0,
        ),
        axis=1, keepdims=True,
    )
    kept = 2 * KMAX // sectors
    slot = lax.broadcasted_iota(jnp.int32, (share, 2 * kept), 1)
    wave = sectors * (jnp.where(slot < kept, slot, slot - kept) - kept // 2)
    for device in range(sectors):
        @pl.when(lon != device)
        def _(device=device):
            pltpu.make_async_remote_copy(
                src_ref=stage.at[device // slices, pl.ds(device % slices * share, share), :],
                dst_ref=spread.at[device], send_sem=a_ss.at[device], recv_sem=a_rs.at[device],
                device_id=(lat, device), device_id_type=pl.DeviceIdType.MESH,
            ).wait()

    def circle(d, k):
        angle = 2.0 * math.pi * ((d * k) % sectors) / sectors
        return math.cos(angle), math.sin(angle)

    even = [spread[0]] + [spread[d] + spread[sectors - d] for d in range(1, half)] + [spread[half]]
    odd = [None] + [spread[d] - spread[sectors - d] for d in range(1, half)]
    blocks = []
    for k in range(half + 1):
        c, s = tw_cos[k : k + 1, :], tw_sin[k : k + 1, :]
        re = weighted([(circle(d, k)[0], even[d]) for d in range(half + 1)])
        im = weighted([(-circle(d, k)[1], odd[d]) for d in range(1, half)])
        if im is None:
            blocks.append(jnp.concatenate([re * c, -(re * s)], axis=1))
        else:
            blocks.append(jnp.concatenate([re * c + im * s, im * c - re * s], axis=1))
    spectrum = jnp.dot(
        jnp.concatenate(blocks, axis=0), fwd[...], precision=HIGHEST, preferred_element_type=jnp.float32
    )
    keep = jnp.concatenate(
        [jnp.where(jnp.abs(wave + k).astype(jnp.float32) <= limit, 1.0, 0.0) for k in range(half + 1)], axis=0
    )
    back = jnp.dot(
        jnp.where(keep > 0.0, spectrum, 0.0), inv[...], precision=HIGHEST, preferred_element_type=jnp.float32
    )
    real, imag = [], []
    for k in range(half + 1):
        c, s = tw_cos[k : k + 1, :], tw_sin[k : k + 1, :]
        zr = back[k * share : (k + 1) * share, :width]
        zi = back[k * share : (k + 1) * share, width:]
        twice = 1.0 if k in (0, half) else 2.0
        real.append((zr * c - zi * s) * twice)
        imag.append((zr * s + zi * c) * twice)
    for d in range(half + 1):
        p = weighted([(circle(d, k)[0], real[k]) for k in range(half + 1)])
        q = weighted([(circle(d, k)[1], imag[k]) for k in range(1, half)])
        if q is None:
            send_b[d] = p
        else:
            send_b[d] = p - q
            send_b[sectors - d] = p + q

    copies = []
    for t in range(1, sectors):
        copy = pltpu.make_async_remote_copy(
            src_ref=send_b.at[sector(t)], dst_ref=recv_b.at[lon],
            send_sem=b_ss.at[t], recv_sem=b_rs.at[t],
            device_id=(lat, sector(t)), device_id_type=pl.DeviceIdType.MESH,
        )
        copy.start()
        copies.append(copy)
    recv_b[lon] = send_b[lon]
    plain = border(filtered, 0), column(filtered, 0), column(filtered, width - 1)
    polar = (lat == 0) | last
    for copy in copies:
        copy.wait()

    cells = recv_b[...].reshape(lev * pole // 8, 8, width)
    order = lax.broadcasted_iota(jnp.int32, cells.shape, 0)
    order = lax.div(order, pole // 8) * per + offset + lax.rem(order, pole // 8)
    mine = order == lax.broadcasted_iota(jnp.int32, cells.shape, 2)
    step = lax.rem(lane8, per) - offset
    fresh = (step >= 0) & (step < pole // 8) & polar

    def renewed(old, at):
        return jnp.where(fresh, jnp.sum(jnp.where(mine, cells[:, :, at : at + 1], 0.0), axis=0), old)

    rim = jnp.concatenate(
        [recv_b[l * slices, 0:1, :] for l in range(lev)]
        + [recv_b[l * slices + slices - 1, share - 1 : share, :] for l in range(lev)],
        axis=0,
    )
    edge = jnp.where(((row8 < lev) & (lat == 0)) | ((row8 >= lev) & last), rim, plain[0])
    first_column, last_column = renewed(plain[1], 0), renewed(plain[2], width - 1)
    copies = post(1, edge, first_column, last_column)
    fixed[0] = tuple(a * b for a, b in zip(fixed[0], (edge, first_column, last_column)))

    def restore(start):
        for l in range(lev):
            for q in range(slices):
                filtered[l, start + q * share : start + (q + 1) * share, :] = recv_b[l * slices + q]

    @pl.when(lat == 0)
    def _():
        restore(0)

    @pl.when(lat == bands - 1)
    def _():
        restore(rows - pole)

    for l in range(lev):
        scaled[l] = filtered[l] * scaled[l]
    chain = [filtered, ping, pong, ping, balanced]
    for sweep in range(SWEEPS):
        turn, source, target = 1 + sweep, chain[sweep], chain[sweep + 1]
        if sweep < SWEEPS - 1:
            second, second_first, second_last = border(source, 1), column(source, 1), column(source, width - 2)
        for copy in copies:
            copy.wait()
        top, bottom = outer(turn)
        if sweep < SWEEPS - 1:
            west, east = col_recv[turn, 0], col_recv[turn, 1]
            around_edge = (
                jnp.where(lane8 == 0, ends(west), pltpu.roll(edge, 1, 1))
                + jnp.where(lane8 == width - 1, ends(east), pltpu.roll(edge, width - 1, 1))
                + jnp.concatenate([top, bottom], axis=0)
                + second
            )
            around_first = west + second_first + along(first_column, top, bottom, 0)
            around_last = east + second_last + along(last_column, top, bottom, width - 1)
            edge, first_column, last_column = [
                a + b * c for a, b, c in zip(*fixed, (around_edge, around_first, around_last))
            ]
            copies = post(turn + 1, edge, first_column, last_column)
        edges = sides(turn, top, bottom)
        for l in range(lev):
            w, e, u, d = around(source, l, edges)
            target[l] = scaled[l] + coupling[l] * (w + e + u + d)


def solution(mesh):
    sectors, bands = mesh.shape["lon"], mesh.shape["lat"]

    def per_device(tracer, wind_east, wind_north, kappa, cutoff, partner):
        lev, rows, width = tracer.shape
        share = lev * (cutoff.shape[0] // 2) // sectors
        turns = SWEEPS + 1
        block = pltpu.VMEM((lev, rows, width), jnp.float32)
        vmem = pl.BlockSpec(memory_space=pltpu.VMEM)
        small = (cutoff.reshape(1, -1), partner.reshape(sectors, width), *tables(sectors, width))
        return pl.pallas_call(
            functools.partial(kernel, sectors, bands),
            out_shape=[jax.ShapeDtypeStruct(tracer.shape, jnp.float32)] * 2,
            in_specs=[pl.BlockSpec(memory_space=pltpu.HBM)] * 10,
            out_specs=[vmem] * 2,
            scratch_shapes=[
                block, block, block, block,
                *[pltpu.VMEM(a.shape, a.dtype) for a in small],
                pltpu.SemaphoreType.DMA((10,)),
                pltpu.VMEM((turns, 2, 8, width), jnp.float32),
                pltpu.VMEM((turns, 2, 8, width), jnp.float32),
                pltpu.VMEM((turns, 2 * lev, width), jnp.float32),
                pltpu.VMEM((turns, 4, 2 * lev, width), jnp.float32),
                pltpu.VMEM((lev, cutoff.shape[0] // 2, width), jnp.float32),
                pltpu.VMEM((sectors, share, width), jnp.float32),
                pltpu.VMEM((sectors, share, width), jnp.float32),
                pltpu.VMEM((sectors, share, width), jnp.float32),
                block, block, block, block,
                pltpu.SemaphoreType.DMA((turns, 6)),
                pltpu.SemaphoreType.DMA((turns, 6)),
                pltpu.SemaphoreType.DMA((sectors,)),
                pltpu.SemaphoreType.DMA((sectors,)),
                pltpu.SemaphoreType.DMA((sectors,)),
                pltpu.SemaphoreType.DMA((sectors,)),
            ],
            compiler_params=pltpu.CompilerParams(
                collective_id=0, has_side_effects=True, vmem_limit_bytes=32 * 1024 * 1024
            ),
        )(
            *[pltpu.with_memory_space_constraint(jnp.asarray(a), pltpu.HBM) for a in (tracer, wind_east, wind_north, kappa, *small)]
        )

    spec = P(None, "lat", "lon")
    return jax.shard_map(
        per_device, mesh=mesh, in_specs=(spec, spec, spec, spec, P(), P()), out_specs=(spec, spec),
        check_vma=False,
    )
```

profile of v0, /device:TPU:0, one launch (start us, length us, event | category | flops | bytes accessed | tf_op | source)
XLA Modules:
  0.0 39.1 jit_solution(9898946697001262657)
XLA Ops:
  0.6 36.9 %shard_map.113 = (f32[4,256,128]{2,1,0:T(8,128)S(1)}, f32[4,256,128]{2,1,0:T(8,128)S(1)}) custom-call(f32[4,256,128]{2,1,0:T(8,128)} %tracer_h.1, f32[4,256,128]{2,1,0:T(8,128)} %wind_east_h.1, f32[4,256,128]{2,1,0:T(8,128)} %wind_north_h.1, f32[4,256,128]{2,1,0:T(8,128)} %kappa_h.1, s32[1,128]{1,0:T(1,128)} %bitcast.3, s32[16,128]{1,0:T(8,128)} %bitcast.2, ...), custom_call_target="tpu_custom_call" | custom-call | tf_op jit(solution)/shard_map/pallas_call | solution.py:386
  37.5 0.8 %copy.14 = f32[4,256,128]{2,1,0:T(8,128)} copy(f32[4,256,128]{2,1,0:T(8,128)S(1)} %get-tuple-element.4) | data formatting | bytes 1048576
  38.3 0.8 %copy.15 = f32[4,256,128]{2,1,0:T(8,128)} copy(f32[4,256,128]{2,1,0:T(8,128)S(1)} %get-tuple-element.5) | data formatting | bytes 1048576
where the time goes:
time: 39.3 us; the launch traced here: 39.1 us
  Pallas kernels  36.9 us (94%)
  local copies, waits for them, and re-layouts  1.59 us (4%)
  between operations  0.64 us (2%)
    pallas_call x1, Pallas kernels, per_device(): pl.pallas_call(functools.partial(kernel, sectors, bands), out_shape=[jax....  36.9 us
    unnamed x2, local copies, waits for them, and re-layouts  1.59 us

commit v1 on v0

v1 whole, which is shorter than its diff:
```python
import functools
import math

import jax
import jax.numpy as jnp
import numpy as np
from jax import lax
from jax.experimental import pallas as pl
from jax.experimental.pallas import tpu as pltpu
from jax.sharding import PartitionSpec as P

KMAX = 512
SWEEPS = 4
COURANT = 0.4
HIGHEST = lax.Precision.HIGHEST


def tables(sectors, width):
    total = sectors * width
    half = sectors // 2
    m = np.arange(width)
    theta = 2.0 * np.pi * (np.outer(np.arange(half + 1), m) % total) / total
    kept = 2 * KMAX // sectors
    k2 = np.arange(kept) - kept // 2
    phase = 2.0 * np.pi * (np.outer(m, k2) % width) / width
    c, s = np.cos(phase), np.sin(phase)
    forward = np.block([[c, -s], [s, c]])
    inverse = np.block([[c.T, s.T], [-s.T, c.T]]) / total
    return [a.astype(np.float32) for a in (np.cos(theta), np.sin(theta), forward, inverse)]


def weighted(terms):
    total = None
    for factor, value in terms:
        if abs(factor) < 1e-12:
            continue
        part = value if abs(factor - 1.0) < 1e-12 else value * np.float32(factor)
        total = part if total is None else total + part
    return total


PAD = 16
DEEP = 24
MESH = pl.DeviceIdType.MESH


def taken(x, at_lane):
    return jnp.take_along_axis(x, at_lane, axis=1, mode="promise_in_bounds")


def kernel(
    sectors, bands,
    tracer_h, wind_east_h, wind_north_h, kappa_h, cutoff_h, partner_h, tw_cos_h, tw_sin_h, fwd_h, inv_h,
    filtered, balanced,
    tr, we, wn, ka, cutoff, partner, tw_cos, tw_sin, fwd, inv, load_s,
    send_a, recv_a, pole_send, pole_recv, send_d, recv_d, cross_send, cross_recv, beyond_fix, strip,
    rim_send, rim_recv, adv_send, adv_recv, kcorner_send, kcorner_recv, corner_send, corner_recv,
    field, ping, pong, invert, coupling, scaled,
    side_tiles, side, side_kappa, side_scaled, side_coupling, side_cross,
    a_ss, a_rs, d_ss, d_rs, b_ss, b_rs, c_ss, c_rs, x_ss, x_rs,
):
    lev, rows, width = we.shape
    pole = cutoff.shape[1] // 2
    share = lev * pole // sectors
    slices = sectors // lev
    half = sectors // 2
    groups = rows // 8
    lat = lax.axis_index("lat")
    lon = lax.axis_index("lon")
    last = lat == bands - 1
    north = lat == 0
    polar = north | last

    def sector(offset):
        return lax.rem(lon + (offset % sectors), sectors)

    def band(offset):
        return lax.rem(lat + (offset % bands), bands)

    barrier = pltpu.get_barrier_semaphore()
    for t in range(1, sectors):
        pl.semaphore_signal(barrier, inc=1, device_id=(lat, sector(t)), device_id_type=MESH)
    beside = (1,) if bands == 2 else (1, -1)
    for t in beside:
        pl.semaphore_signal(barrier, inc=1, device_id=(band(t), lon), device_id_type=MESH)

    body = pl.ds(PAD, rows)
    held = (tracer_h, wind_east_h, wind_north_h, kappa_h, partner_h, cutoff_h, tw_cos_h, tw_sin_h, fwd_h, inv_h)
    near = (tr.at[:, body, :], we, wn, ka.at[:, body, :], partner, cutoff, tw_cos, tw_sin, fwd, inv)
    loads = [pltpu.make_async_copy(h, v, load_s.at[i]) for i, (h, v) in enumerate(zip(held, near))]
    for load in loads:
        load.start()

    lane = lax.broadcasted_iota(jnp.int32, (8, width), 1)
    row8 = lax.broadcasted_iota(jnp.int32, (8, width), 0)
    zero = jnp.zeros((8, width), jnp.float32)

    def roll(x, by):
        by = by % width
        return x if by == 0 else pltpu.roll(x, by, 1)

    def swapped(v0, v1):
        low = lane < width // 2
        v0, v1 = jnp.where(low, v0, roll(v1, width // 2)), jnp.where(low, roll(v0, width // 2), v1)
        out = []
        for v in (v0, v1):
            for b in (2, 1, 0):
                step, hop = 1 << b, 8 << b
                upper = (lane & hop) != 0
                same = ((row8 >> b) & 1) == ((lane >> (3 + b)) & 1)
                v = jnp.where(
                    same, v,
                    jnp.where(upper, pltpu.roll(roll(v, hop), 8 - step, 0), pltpu.roll(roll(v, -hop), step, 0)),
                )
            out.append(v)
        return out

    base = pl.multiple_of(jnp.where(last, rows - pole, 0), 8)
    tip = jnp.where(last, rows - 1, 0)
    tip_tile = pl.multiple_of(jnp.where(last, rows - 8, 0), 8)
    tip_slice = jnp.where(last, slices - 1, 0)
    keeper = lax.rem(lon, slices) == tip_slice

    @pl.when(north)
    def _():
        for l in range(lev):
            tr[l, PAD - 8 : PAD, :] = zero

    @pl.when(last)
    def _():
        for l in range(lev):
            tr[l, PAD + rows : PAD + rows + 8, :] = zero

    for load in loads[:3]:
        load.wait()
    lane_p = lax.broadcasted_iota(jnp.int32, (pole, width), 1)
    row_p = lax.broadcasted_iota(jnp.int32, (pole, width), 0)
    before = jnp.where(last, rows - pole - 1, 0)
    after = jnp.where(last, rows - 1, pole)
    eight = lane & 7
    packs = [zero, zero]
    for l in range(lev):
        x = tr[l, pl.ds(base + PAD, pole), :]
        east_wind = we[l, pl.ds(base, pole), :]
        w = jnp.where(lane_p == 0, 0.0, pltpu.roll(x, 1, 1))
        e = jnp.where(lane_p == width - 1, 0.0, pltpu.roll(x, width - 1, 1))
        above = jnp.where(last, tr[l, pl.ds(PAD + before, 1), :], 0.0)
        below = jnp.where(last, 0.0, tr[l, pl.ds(PAD + after, 1), :])
        u = jnp.where(row_p == 0, above, pltpu.roll(x, 1, 0))
        d = jnp.where(row_p == pole - 1, below, pltpu.roll(x, pole - 1, 0))
        stage = x - COURANT * 0.5 * (east_wind * (e - w) + wn[l, pl.ds(base, pole), :] * (d - u))
        for q in range(slices):
            k = l * slices + q
            send_a[k * DEEP : k * DEEP + share, :] = stage[q * share : (q + 1) * share]
            for h in range(2):
                at = q * share + 8 * h
                t = jnp.where(
                    (eight == 3) | (eight == 4), roll(x[at : at + 8], 4 + 8 * k), roll(east_wind[at : at + 8], 6 + 8 * k)
                )
                packs[h] = jnp.where((lane >> 3) == k, t, packs[h])
    for h, v in enumerate(swapped(*packs)):
        for k in range(8):
            send_a[(8 * h + k) * DEEP + share : (8 * h + k) * DEEP + share + 1, :] = v[k : k + 1]

    pl.semaphore_wait(barrier, sectors - 1 + len(beside))

    def across(src, dst, stride, count, ss, rs):
        copies = []
        for t in range(1, sectors):
            copies.append(
                pltpu.make_async_remote_copy(
                    src_ref=src.at[pl.ds(pl.multiple_of(sector(t) * stride, 8), count), :],
                    dst_ref=dst.at[pl.ds(pl.multiple_of(lon * stride, 8), count), :],
                    send_sem=ss.at[t], recv_sem=rs.at[t], device_id=(lat, sector(t)), device_id_type=MESH,
                )
            )
        return copies

    a_copies = across(send_a, recv_a, DEEP, share + 1, a_ss, a_rs)
    for copy in a_copies:
        copy.start()

    loads[3].wait()
    for l in range(lev):
        pole_send[16 * l : 16 * l + 8, :] = ka[l, pl.ds(tip_tile + PAD, 8), :]
        pole_send[16 * l + 8 : 16 * l + 9, :] = tr[l, pl.ds(tip + PAD, 1), :]
        pole_send[16 * l + 9 : 16 * l + 10, :] = wn[l, pl.ds(tip, 1), :]

    def pole_copy(l):
        return pltpu.make_async_remote_copy(
            src_ref=pole_send.at[pl.ds(16 * l, 10), :], dst_ref=pole_recv.at[pl.ds(pl.multiple_of(16 * lon, 8), 10), :],
            send_sem=b_ss.at[l], recv_sem=b_rs.at[lon],
            device_id=(lat, l * slices + tip_slice), device_id_type=MESH,
        )

    for l in range(lev):
        @pl.when(lon != l * slices + tip_slice)
        def _(l=l):
            pole_copy(l).start()

        @pl.when(lon == l * slices + tip_slice)
        def _(l=l):
            pole_recv[pl.ds(pl.multiple_of(16 * lon, 8), 8), :] = pole_send[16 * l : 16 * l + 8, :]
            pole_recv[pl.ds(pl.multiple_of(16 * lon, 8) + 8, 2), :] = pole_send[16 * l + 8 : 16 * l + 10, :]

    four = lane >> 2

    def packed(tiles):
        first, second = zero, zero
        for g, x in enumerate(tiles):
            z = roll(x, 4 * g + 4)
            first = jnp.where(four == g, z, first)
            second = jnp.where(four == (g + 1) % groups, z, second)
        return first, second

    def pack_rims(l, carry):
        at = pl.multiple_of(8 * l, 8)
        for i, source in enumerate((tr, ka)):
            first, second = packed([source[l, PAD + 8 * g : PAD + 8 * g + 8, :] for g in range(groups)])
            rim_send[0, pl.ds(at + 8 * lev * i, 8), :] = first
            rim_send[1, pl.ds(at + 8 * lev * i, 8), :] = second
        return carry

    lax.fori_loop(0, lev, pack_rims, 0)

    def sideways(src, dst, i):
        return [
            pltpu.make_async_remote_copy(
                src_ref=src.at[j], dst_ref=dst.at[j], send_sem=x_ss.at[i + j], recv_sem=x_rs.at[i + j],
                device_id=(lat, sector(1 - 2 * j)), device_id_type=MESH,
            )
            for j in range(2)
        ]

    class Polewards:
        def __init__(self, step, src, dst, i):
            self.copy = lambda: pltpu.make_async_remote_copy(
                src_ref=src, dst_ref=dst, send_sem=x_ss.at[i], recv_sem=x_rs.at[i],
                device_id=(band(step), lon), device_id_type=MESH,
            )
            self.sends = lat < bands - 1 if step == 1 else lat > 0
            self.takes = lat > 0 if step == 1 else lat < bands - 1

        def start(self):
            @pl.when(self.sends)
            def _():
                self.copy().start()

        def wait_recv(self):
            @pl.when(self.takes)
            def _():
                self.copy().wait_recv()

        def wait_send(self):
            @pl.when(self.sends)
            def _():
                self.copy().wait_send()

    def over_rows(ref, i):
        return [
            Polewards(1, ref.at[:, pl.ds(PAD + rows - 8, 8), :], ref.at[:, pl.ds(PAD - 8, 8), :], i),
            Polewards(-1, ref.at[:, pl.ds(PAD, 8), :], ref.at[:, pl.ds(PAD + rows, 8), :], i + 1),
        ]

    x0 = sideways(rim_send, rim_recv, 0) + over_rows(tr, 2) + over_rows(ka, 4)
    for copy in x0:
        copy.start()
    for load in loads[4:]:
        load.wait()

    start = lax.broadcasted_iota(jnp.int32, (sectors, width), 0) + half
    reach = partner[...] - jnp.where(start >= sectors, start - sectors, start) * width
    reach = jnp.where(reach < 0, reach + sectors * width, reach)
    farther = reach >= width
    at_lane = jnp.where(farther, reach - width, reach)

    def crossed(points):
        return jnp.where(
            farther, taken(pltpu.roll(points, sectors - half - 1, 0), at_lane), taken(pltpu.roll(points, half, 0), at_lane)
        )

    for copy in x0:
        copy.wait_recv()

    def renew(l, carry):
        at = pl.multiple_of(8 * l, 8)
        rim = jnp.where(
            (lane & 3) == 3, rim_recv[0, pl.ds(at, 8), :], roll(rim_recv[1, pl.ds(at, 8), :], -2)
        )
        tiles = []
        for g in range(groups):
            at = PAD + 8 * g
            x = tr[l, at : at + 8, :]
            h = roll(rim, -(4 * g + 3))
            w = jnp.where(lane == 0, h, roll(x, 1))
            e = jnp.where(lane == width - 1, h, roll(x, -1))
            turn = wn[l, 8 * g : 8 * g + 8, :] * (tr[l, at + 1 : at + 9, :] - tr[l, at - 1 : at + 7, :])
            value = x - COURANT * 0.5 * (we[l, 8 * g : 8 * g + 8, :] * (e - w) + turn)
            field[l, at : at + 8, :] = value
            filtered[l, 8 * g : 8 * g + 8, :] = value
            k = ka[l, at : at + 8, :]
            inverse = 1.0 / (1.0 + 4.0 * k)
            invert[l, at : at + 8, :] = inverse
            coupling[l, at : at + 8, :] = k * inverse
            scaled[l, at : at + 8, :] = value * inverse
            tiles.append(value)
        first, second = packed(tiles)
        at = pl.multiple_of(8 * l, 8)
        adv_send[0, pl.ds(at, 8), :] = first
        adv_send[1, pl.ds(at, 8), :] = second
        for at in (PAD - 8, PAD + rows):
            k = ka[l, at : at + 8, :]
            inverse = 1.0 / (1.0 + 4.0 * k)
            invert[l, at : at + 8, :] = inverse
            coupling[l, at : at + 8, :] = k * inverse
        return carry

    lax.fori_loop(0, lev, renew, 0)

    def sided(send, recv, at, put):
        for kk in range(4):
            mine = (four & 3) == kk
            near_west = jnp.where(mine, recv[0, at : at + 8, :], send[1, at : at + 8, :])
            near_east = jnp.where(mine, send[0, at : at + 8, :], recv[1, at : at + 8, :])
            put(kk, jnp.where((lane & 15) < 8, roll(near_west, -4 * kk), roll(near_east, 8 - 4 * kk)))

    for l in range(lev):
        def put(kk, tile, l=l):
            side_kappa[l, 12 + 8 * kk : 20 + 8 * kk, :] = tile
            if kk == 3:
                kcorner_send[0, 8 * l : 8 * l + 8, :] = tile
            if kk == 0:
                kcorner_send[1, 8 * l : 8 * l + 8, :] = tile

        sided(rim_send, rim_recv, 8 * (lev + l), put)

    def corners(send, recv, i):
        return [Polewards(1, send.at[0], recv.at[0], i), Polewards(-1, send.at[1], recv.at[1], i + 1)]

    x1 = sideways(adv_send, adv_recv, 6) + over_rows(field, 8) + corners(kcorner_send, kcorner_recv, 10)
    for copy in x1:
        copy.start()

    beyond_fix[...] = jnp.zeros_like(beyond_fix)

    @pl.when(keeper)
    def _():
        for d in range(sectors):
            @pl.when(lon != d)
            def _(d=d):
                pltpu.make_async_remote_copy(
                    src_ref=pole_send.at[pl.ds(0, 10), :], dst_ref=pole_recv.at[pl.ds(16 * d, 10), :],
                    send_sem=b_ss.at[0], recv_sem=b_rs.at[d], device_id=(lat, sector(1)), device_id_type=MESH,
                ).wait_recv()
        tips = jnp.concatenate([pole_recv[16 * d + 8 : 16 * d + 9, :] for d in range(sectors)], axis=0)
        winds = jnp.concatenate([pole_recv[16 * d + 9 : 16 * d + 10, :] for d in range(sectors)], axis=0)
        turned = COURANT * 0.5 * winds * crossed(tips)
        beyond_fix[...] = jnp.where(last, -turned, turned)

    first = jnp.where(last, pole, 0) + lax.rem(lon, slices) * share
    spot = lax.broadcasted_iota(jnp.int32, (share, 2 * pole), 0) + first
    limit = jnp.sum(
        jnp.where(
            lax.broadcasted_iota(jnp.int32, (share, 2 * pole), 1) == spot,
            cutoff[...].astype(jnp.float32), 0.0,
        ),
        axis=1, keepdims=True,
    )
    kept = 2 * KMAX // sectors
    slot = lax.broadcasted_iota(jnp.int32, (share, 2 * kept), 1)
    wave = sectors * (jnp.where(slot < kept, slot, slot - kept) - kept // 2)
    own = pl.multiple_of(lon * DEEP, 8)
    recv_a[pl.ds(own, share), :] = send_a[pl.ds(own, share), :]
    recv_a[pl.ds(own + share, 1), :] = send_a[pl.ds(own + share, 1), :]
    for copy in a_copies:
        copy.wait_recv()

    def rows_of(ref):
        return [
            jnp.concatenate(
                [ref[(8 * h + k) * DEEP + share : (8 * h + k) * DEEP + share + 1, :] for k in range(8)], axis=0
            )
            for h in range(2)
        ]

    fixes = []
    for v in swapped(*rows_of(recv_a)):
        fixes.append(COURANT * 0.5 * v * jnp.where(eight == 6, roll(v, 11), -roll(v, -7)))
    at_tip = [(row8 == 0) & north & keeper, (row8 == 7) & last & keeper]
    ends = (lane == 0) | (lane == width - 1)
    spread = []
    for d in range(sectors):
        parts = []
        for h in range(2):
            x = recv_a[d * DEEP + 8 * h : d * DEEP + 8 * h + 8, :]
            x = x + jnp.where(ends, roll(fixes[h], -(8 * d + 6)), 0.0)
            parts.append(x + jnp.where(at_tip[h], beyond_fix[d : d + 1, :], 0.0))
        spread.append(jnp.concatenate(parts, axis=0))

    def circle(d, k):
        angle = 2.0 * math.pi * ((d * k) % sectors) / sectors
        return math.cos(angle), math.sin(angle)

    even = [spread[0]] + [spread[d] + spread[sectors - d] for d in range(1, half)] + [spread[half]]
    odd = [None] + [spread[d] - spread[sectors - d] for d in range(1, half)]
    blocks = []
    for k in range(half + 1):
        c, s = tw_cos[k : k + 1, :], tw_sin[k : k + 1, :]
        re = weighted([(circle(d, k)[0], even[d]) for d in range(half + 1)])
        im = weighted([(-circle(d, k)[1], odd[d]) for d in range(1, half)])
        if im is None:
            blocks.append(jnp.concatenate([re * c, -(re * s)], axis=1))
        else:
            blocks.append(jnp.concatenate([re * c + im * s, im * c - re * s], axis=1))
    spectrum = jnp.dot(
        jnp.concatenate(blocks, axis=0), fwd[...], precision=HIGHEST, preferred_element_type=jnp.float32
    )
    keep = jnp.concatenate(
        [jnp.where(jnp.abs(wave + k).astype(jnp.float32) <= limit, 1.0, 0.0) for k in range(half + 1)], axis=0
    )
    back = jnp.dot(
        jnp.where(keep > 0.0, spectrum, 0.0), inv[...], precision=HIGHEST, preferred_element_type=jnp.float32
    )
    real, imag = [], []
    for k in range(half + 1):
        c, s = tw_cos[k : k + 1, :], tw_sin[k : k + 1, :]
        zr = back[k * share : (k + 1) * share, :width]
        zi = back[k * share : (k + 1) * share, width:]
        twice = 1.0 if k in (0, half) else 2.0
        real.append((zr * c - zi * s) * twice)
        imag.append((zr * s + zi * c) * twice)
    smooth = [None] * sectors
    for d in range(half + 1):
        p = weighted([(circle(d, k)[0], real[k]) for k in range(half + 1)])
        q = weighted([(circle(d, k)[1], imag[k]) for k in range(1, half)])
        if q is None:
            smooth[d] = p
        else:
            smooth[d], smooth[sectors - d] = p - q, p + q
    edges = [zero, zero]
    for d in range(sectors):
        send_d[d * DEEP : d * DEEP + share, :] = smooth[d]
        for h in range(2):
            edges[h] = jnp.where((lane >> 3) == d, roll(smooth[d][8 * h : 8 * h + 8], 8 * d + 4), edges[h])
    edges = [jnp.where(eight < 4, roll(v, 8), roll(v, -8)) for v in edges]
    for h, v in enumerate(swapped(*edges)):
        for k in range(8):
            send_d[(8 * h + k) * DEEP + share : (8 * h + k) * DEEP + share + 1, :] = v[k : k + 1]

    d_copies = across(send_d, recv_d, DEEP, share + 1, d_ss, d_rs)
    for copy in d_copies:
        copy.start()
    recv_d[pl.ds(own, share), :] = send_d[pl.ds(own, share), :]
    recv_d[pl.ds(own + share, 1), :] = send_d[pl.ds(own + share, 1), :]

    me = lax.div(lon, slices)

    def cross_copy(d):
        return pltpu.make_async_remote_copy(
            src_ref=cross_send.at[pl.ds(8 * d, 5), :], dst_ref=cross_recv.at[pl.ds(pl.multiple_of(8 * me, 8), 5), :],
            send_sem=c_ss.at[d], recv_sem=c_rs.at[me], device_id=(lat, d), device_id_type=MESH,
        )

    @pl.when(keeper)
    def _():
        now, inverse, pull = [], [], []
        for d in range(sectors):
            top, low = d * DEEP, d * DEEP + 8
            now.append(jnp.where(last, send_d[low : low + 8, :], send_d[top : top + 8, :]))
            k = pole_recv[16 * d : 16 * d + 8, :]
            inverse.append(1.0 / (1.0 + 4.0 * k))
            pull.append(k * inverse[d])
        source = [a * b for a, b in zip(now, inverse)]
        ends = jnp.zeros((sectors, width), jnp.float32)
        wide = lax.broadcasted_iota(jnp.int32, (sectors, width), 1)
        for t in range(SWEEPS):
            tips = jnp.concatenate([jnp.where(last, x[7:8], x[0:1]) for x in now], axis=0)
            over = crossed(tips)
            for d in range(sectors):
                cross_send[8 * d + t : 8 * d + t + 1, :] = over[d : d + 1]
            z = roll(over, 8 * t + 4)
            z = jnp.where((wide & 7) < 4, pltpu.roll(z, 1, 0), pltpu.roll(z, sectors - 1, 0))
            ends = jnp.where((wide >> 3) == t, z, ends)
            if t < SWEEPS - 1:
                right, left = [roll(x, 1) for x in now], [roll(x, -1) for x in now]
                later = []
                for d in range(sectors):
                    w = jnp.where(lane == 0, right[d - 1], right[d])
                    e = jnp.where(lane == width - 1, left[(d + 1) % sectors], left[d])
                    u = jnp.where((row8 == 0) & jnp.logical_not(last), over[d : d + 1], pltpu.roll(now[d], 1, 0))
                    b = jnp.where((row8 == 7) & last, over[d : d + 1], pltpu.roll(now[d], 7, 0))
                    later.append(source[d] + pull[d] * (w + e + u + b))
                now = later
        for d in range(sectors):
            cross_send[8 * d + 4 : 8 * d + 5, :] = ends[d : d + 1]
        for d in range(sectors):
            @pl.when(lon != d)
            def _(d=d):
                cross_copy(d).start()
        cross_recv[pl.ds(pl.multiple_of(8 * me, 8), 5), :] = cross_send[pl.ds(pl.multiple_of(8 * lon, 8), 5), :]

    for copy in x1:
        copy.wait_recv()
    for l in range(lev):
        def put(kk, tile, l=l):
            side_tiles[32 * l + 8 * kk : 32 * l + 8 * kk + 8, :] = tile
            if kk == 3:
                corner_send[0, 8 * l : 8 * l + 8, :] = tile
            if kk == 0:
                corner_send[1, 8 * l : 8 * l + 8, :] = tile

        sided(adv_send, adv_recv, 8 * l, put)
    x2 = corners(corner_send, corner_recv, 12)
    for copy in x2:
        copy.start()

    def capped(first_tile, last_tile, recv, l):
        top = roll(jnp.where(lane < width - 16, last_tile, recv[0, 8 * l : 8 * l + 8, :]), 16)
        bottom = roll(jnp.where(lane >= 16, first_tile, recv[1, 8 * l : 8 * l + 8, :]), -16)
        return top, bottom

    for l in range(lev):
        top, bottom = capped(kcorner_send[1, 8 * l : 8 * l + 8, :], kcorner_send[0, 8 * l : 8 * l + 8, :], kcorner_recv, l)
        side_kappa[l, 4:12, :] = top
        side_kappa[l, 44:52, :] = bottom
        for j in range(5):
            at = 8 + 8 * j
            k = side_kappa[l, at : at + 8, :]
            inverse = 1.0 / (1.0 + 4.0 * k)
            side_kappa[l, at : at + 8, :] = inverse
            side_coupling[l, at : at + 8, :] = k * inverse
        for at in (PAD - 8, PAD + rows):
            scaled[l, at : at + 8, :] = field[l, at : at + 8, :] * invert[l, at : at + 8, :]
    for copy in x2:
        copy.wait_recv()

    for copy in d_copies:
        copy.wait_recv()
    for l in range(lev):
        @pl.when(lon != l * slices + tip_slice)
        def _(l=l):
            pltpu.make_async_remote_copy(
                src_ref=cross_send.at[pl.ds(0, 5), :], dst_ref=cross_recv.at[pl.ds(8 * l, 5), :],
                send_sem=c_ss.at[0], recv_sem=c_rs.at[l], device_id=(lat, sector(1)), device_id_type=MESH,
            ).wait_recv()

    @pl.when(polar)
    def _():
        for k in range(sectors):
            l, q = k // slices, k % slices
            x = recv_d[k * DEEP : k * DEEP + share, :]
            at = base + PAD + q * share
            field[l, pl.ds(at, share), :] = x
            scaled[l, pl.ds(at, share), :] = x * invert[l, pl.ds(at, share), :]
            filtered[l, pl.ds(base + q * share, share), :] = x

    def set_cross(target, t):
        @pl.when(north)
        def _():
            for l in range(lev):
                target[l, PAD - 1 : PAD, :] = cross_recv[8 * l + t : 8 * l + t + 1, :]

        @pl.when(last)
        def _():
            for l in range(lev):
                target[l, PAD + rows : PAD + rows + 1, :] = cross_recv[8 * l + t : 8 * l + t + 1, :]

    set_cross(field, 0)

    halo = jnp.concatenate([cross_recv[8 * l + 4 : 8 * l + 5, :] for l in range(lev)] * 2, axis=0)
    for t in range(SWEEPS):
        plain = jnp.concatenate([cross_recv[8 * l + t : 8 * l + t + 1, :] for l in range(lev)] * 2, axis=0)
        z = jnp.where(
            lane < 8,
            jnp.where(lane < 4, roll(halo, -8 * t), roll(plain, 4)),
            jnp.where(lane < 12, roll(plain, 12), roll(halo, 8 - 8 * t)),
        )
        side_cross[t] = jnp.where(last, roll(z, -16), z)

    outside = [jnp.where(last, roll(v, 96), v) for v in swapped(*rows_of(recv_d))]
    from_cap = jnp.where(last, lane - (width - 32), lane)
    inside_cap = polar & (from_cap >= 0) & (from_cap < 32)
    top_spot = north & (row8 == 7) & (lane < 16)
    bottom_spot = last & (row8 == 0) & (lane >= width - 16)
    for l in range(lev):
        tiles = []
        for kk in range(4):
            z = zero
            for g in range(2):
                k, h = l * slices + 2 * g + kk // 2, kk % 2
                x = recv_d[k * DEEP + 8 * h : k * DEEP + 8 * h + 8, :]
                part = lane - 16 * g
                inner = jnp.where(part < 8, roll(x, 16 * g + 4), roll(x, 16 * g + 12))
                inner = jnp.where(last, roll(inner, 96), inner)
                z_outer = outside[h]
                here = from_cap - 16 * g
                outer = jnp.where(here < 8, roll(z_outer, 16 * g - 8 * k), roll(z_outer, 16 * g + 8 - 8 * k))
                value = jnp.where((here >= 4) & (here < 12), inner, outer)
                z = jnp.where((here >= 0) & (here < 16), value, z)
            tile = jnp.where(inside_cap, z, side_tiles[32 * l + 8 * kk : 32 * l + 8 * kk + 8, :])
            side[0, l, 12 + 8 * kk : 20 + 8 * kk, :] = tile
            tiles.append(tile)
        top, bottom = capped(tiles[0], tiles[3], corner_recv, l)
        side[0, l, 4:12, :] = jnp.where(top_spot, side_cross[0, l : l + 1, :], top)
        side[0, l, 44:52, :] = jnp.where(bottom_spot, side_cross[0, l : l + 1, :], bottom)

    for t in range(SWEEPS - 1):
        for l in range(lev):
            for j in range(5):
                at = 8 + 8 * j
                x = side[t, l, at : at + 8, :]
                total = roll(x, 1) + roll(x, -1) + side[t, l, at - 1 : at + 7, :] + side[t, l, at + 1 : at + 9, :]
                if t == 0:
                    source = x * side_kappa[l, at : at + 8, :]
                    side_scaled[l, at : at + 8, :] = source
                else:
                    source = side_scaled[l, at : at + 8, :]
                x = source + side_coupling[l, at : at + 8, :] * total
                if j == 0:
                    x = jnp.where(north & (row8 == 3) & (lane < 16), side_cross[t + 1, l : l + 1, :], x)
                if j == 4:
                    x = jnp.where(last & (row8 == 4) & (lane >= width - 16), side_cross[t + 1, l : l + 1, :], x)
                side[t + 1, l, at : at + 8, :] = x

    chain = [field, ping, pong, ping, balanced]
    for sweep in range(SWEEPS):
        source, target = chain[sweep], chain[sweep + 1]
        final = sweep == SWEEPS - 1

        def relax(l, carry, sweep=sweep, source=source, target=target, final=final):
            for kk in range(4) if final else range(-1, 5):
                h = side[sweep, l, 12 + 8 * kk : 20 + 8 * kk, :]
                h = jnp.where((lane & 15) == 3, h, roll(h, -10))
                for g in range(groups // 4) if 0 <= kk < 4 else ((0,) if kk < 0 else (groups // 4 - 1,)):
                    at = PAD + 32 * g + 8 * kk
                    edge = roll(h, -(16 * g + 3))
                    x = source[l, at : at + 8, :]
                    w = jnp.where(lane == 0, edge, roll(x, 1))
                    e = jnp.where(lane == width - 1, edge, roll(x, -1))
                    total = (w + e) + (source[l, at - 1 : at + 7, :] + source[l, at + 1 : at + 9, :])
                    value = scaled[l, at : at + 8, :] + coupling[l, at : at + 8, :] * total
                    put = at - PAD if final else at
                    target[l, put : put + 8, :] = value
            return carry

        lax.fori_loop(0, lev, relax, 0)
        if not final:
            set_cross(target, sweep + 1)

    for copy in a_copies + x0 + x1 + d_copies + x2:
        copy.wait_send()
    for l in range(lev):
        @pl.when(lon != l * slices + tip_slice)
        def _(l=l):
            pole_copy(l).wait_send()

    @pl.when(keeper)
    def _():
        for d in range(sectors):
            @pl.when(lon != d)
            def _(d=d):
                cross_copy(d).wait_send()


def solution(mesh):
    sectors, bands = mesh.shape["lon"], mesh.shape["lat"]

    def per_device(tracer, wind_east, wind_north, kappa, cutoff, partner):
        lev, rows, width = tracer.shape
        f32 = jnp.float32
        block = pltpu.VMEM((lev, rows, width), f32)
        tall = pltpu.VMEM((lev, rows + 2 * PAD, width), f32)
        strips = pltpu.VMEM((sectors * DEEP, width), f32)
        pair = pltpu.VMEM((2, lev * 8, width), f32)
        narrow = pltpu.VMEM((lev, 56, width), f32)
        vmem = pl.BlockSpec(memory_space=pltpu.VMEM)
        small = (cutoff.reshape(1, -1), partner.reshape(sectors, width), *tables(sectors, width))
        dma = pltpu.SemaphoreType.DMA
        return pl.pallas_call(
            functools.partial(kernel, sectors, bands),
            out_shape=[jax.ShapeDtypeStruct(tracer.shape, f32)] * 2,
            in_specs=[pl.BlockSpec(memory_space=pltpu.HBM)] * 10,
            out_specs=[vmem] * 2,
            scratch_shapes=[
                tall, block, block, tall,
                pltpu.VMEM((1, cutoff.shape[0]), jnp.int32), pltpu.VMEM((sectors, width), jnp.int32),
                *[pltpu.VMEM(a.shape, a.dtype) for a in small[2:]],
                dma((10,)),
                strips, strips,
                pltpu.VMEM((16 * lev, width), f32), pltpu.VMEM((16 * sectors, width), f32),
                strips, strips,
                pltpu.VMEM((8 * sectors, width), f32), pltpu.VMEM((8 * lev, width), f32),
                pltpu.VMEM((sectors, width), f32), pltpu.VMEM((8 * sectors, width), f32),
                pltpu.VMEM((2, 2 * lev * 8, width), f32), pltpu.VMEM((2, 2 * lev * 8, width), f32),
                pair, pair, pair, pair, pair, pair,
                tall, tall, tall, tall, tall, tall,
                pltpu.VMEM((lev * 32, width), f32), pltpu.VMEM((SWEEPS, lev, 56, width), f32),
                narrow, narrow, narrow, pltpu.VMEM((SWEEPS, 8, width), f32),
                *[dma((sectors,))] * 4,
                dma((lev,)), dma((sectors,)), dma((sectors,)), dma((lev,)), dma((14,)), dma((14,)),
            ],
            compiler_params=pltpu.CompilerParams(
                collective_id=0, has_side_effects=True, vmem_limit_bytes=32 * 1024 * 1024
            ),
        )(
            *[pltpu.with_memory_space_constraint(jnp.asarray(a), pltpu.HBM) for a in (tracer, wind_east, wind_north, kappa, *small)]
        )

    spec = P(None, "lat", "lon")
    return jax.shard_map(
        per_device, mesh=mesh, in_specs=(spec, spec, spec, spec, P(), P()), out_specs=(spec, spec),
        check_vma=False,
    )
```

time: 39.3 us -> 28.5 us (0.73)
  Pallas kernels: 36.9 us -> 26.1 us
    pallas_call x1, Pallas kernels: 36.9 us -> 26.1 us  [per_device(): pl.pallas_call(functools.partial(kernel, sectors, bands), out_shape=[jax....]
where the time goes in v1:
time: 28.5 us; the launch traced here: 28.4 us
  Pallas kernels  26.1 us (92%)
  local copies, waits for them, and re-layouts  1.59 us (6%)
  between operations  0.64 us (2%)
    pallas_call x1, Pallas kernels, per_device(): pl.pallas_call(functools.partial(kernel, sectors, bands), out_shape=[jax....  26.1 us
    unnamed x2, local copies, waits for them, and re-layouts  1.59 us

profile of v1, /device:TPU:0, one launch (start us, length us, event | category | flops | bytes accessed | tf_op | source)
XLA Modules:
  0.0 28.4 jit_solution(1028725106293553573)
XLA Ops:
  0.6 26.1 %shard_map.113 = (f32[4,256,128]{2,1,0:T(8,128)S(1)}, f32[4,256,128]{2,1,0:T(8,128)S(1)}) custom-call(f32[4,256,128]{2,1,0:T(8,128)} %tracer_h.1, f32[4,256,128]{2,1,0:T(8,128)} %wind_east_h.1, f32[4,256,128]{2,1,0:T(8,128)} %wind_north_h.1, f32[4,256,128]{2,1,0:T(8,128)} %kappa_h.1, s32[1,128]{1,0:T(1,128)} %bitcast.3, s32[16,128]{1,0:T(8,128)} %bitcast.2, ...), custom_call_target="tpu_custom_call" | custom-call | tf_op jit(solution)/shard_map/pallas_call | solution.py:679
  26.8 0.8 %copy.14 = f32[4,256,128]{2,1,0:T(8,128)} copy(f32[4,256,128]{2,1,0:T(8,128)S(1)} %get-tuple-element.4) | data formatting | bytes 1048576
  27.6 0.8 %copy.15 = f32[4,256,128]{2,1,0:T(8,128)} copy(f32[4,256,128]{2,1,0:T(8,128)S(1)} %get-tuple-element.5) | data formatting | bytes 1048576

commit v2 on v1

--- a/solution.py
+++ b/solution.py
@@ -51,12 +51,10 @@
 def kernel(
     sectors, bands,
     tracer_h, wind_east_h, wind_north_h, kappa_h, cutoff_h, partner_h, tw_cos_h, tw_sin_h, fwd_h, inv_h,
-    filtered, balanced,
+    field, scaled, coupling, side, side_scaled, side_coupling, side_cross,
     tr, we, wn, ka, cutoff, partner, tw_cos, tw_sin, fwd, inv, load_s,
-    send_a, recv_a, pole_send, pole_recv, send_d, recv_d, cross_send, cross_recv, beyond_fix, strip,
-    rim_send, rim_recv, adv_send, adv_recv, kcorner_send, kcorner_recv, corner_send, corner_recv,
-    field, ping, pong, invert, coupling, scaled,
-    side_tiles, side, side_kappa, side_scaled, side_coupling, side_cross,
+    send_a, recv_a, pole_send, pole_recv, send_d, recv_d, cross_send, cross_recv, beyond_fix,
+    rim_send, rim_recv, kap_send, kap_recv, kap_diag, adv_send, adv_recv, adv_diag, corner, invert, side_tiles, side_invert,
     a_ss, a_rs, d_ss, d_rs, b_ss, b_rs, c_ss, c_rs, x_ss, x_rs,
 ):
     lev, rows, width = we.shape
@@ -82,7 +80,8 @@
         pl.semaphore_signal(barrier, inc=1, device_id=(lat, sector(t)), device_id_type=MESH)
     beside = (1,) if bands == 2 else (1, -1)
     for t in beside:
-        pl.semaphore_signal(barrier, inc=1, device_id=(band(t), lon), device_id_type=MESH)
+        for i in (-1, 0, 1):
+            pl.semaphore_signal(barrier, inc=1, device_id=(band(t), sector(i)), device_id_type=MESH)
 
     body = pl.ds(PAD, rows)
     held = (tracer_h, wind_east_h, wind_north_h, kappa_h, partner_h, cutoff_h, tw_cos_h, tw_sin_h, fwd_h, inv_h)
@@ -162,7 +161,7 @@
         for k in range(8):
             send_a[(8 * h + k) * DEEP + share : (8 * h + k) * DEEP + share + 1, :] = v[k : k + 1]
 
-    pl.semaphore_wait(barrier, sectors - 1 + len(beside))
+    pl.semaphore_wait(barrier, sectors - 1 + 3 * len(beside))
 
     def across(src, dst, stride, count, ss, rs):
         copies = []
@@ -180,29 +179,6 @@
     for copy in a_copies:
         copy.start()
 
-    loads[3].wait()
-    for l in range(lev):
-        pole_send[16 * l : 16 * l + 8, :] = ka[l, pl.ds(tip_tile + PAD, 8), :]
-        pole_send[16 * l + 8 : 16 * l + 9, :] = tr[l, pl.ds(tip + PAD, 1), :]
-        pole_send[16 * l + 9 : 16 * l + 10, :] = wn[l, pl.ds(tip, 1), :]
-
-    def pole_copy(l):
-        return pltpu.make_async_remote_copy(
-            src_ref=pole_send.at[pl.ds(16 * l, 10), :], dst_ref=pole_recv.at[pl.ds(pl.multiple_of(16 * lon, 8), 10), :],
-            send_sem=b_ss.at[l], recv_sem=b_rs.at[lon],
-            device_id=(lat, l * slices + tip_slice), device_id_type=MESH,
-        )
-
-    for l in range(lev):
-        @pl.when(lon != l * slices + tip_slice)
-        def _(l=l):
-            pole_copy(l).start()
-
-        @pl.when(lon == l * slices + tip_slice)
-        def _(l=l):
-            pole_recv[pl.ds(pl.multiple_of(16 * lon, 8), 8), :] = pole_send[16 * l : 16 * l + 8, :]
-            pole_recv[pl.ds(pl.multiple_of(16 * lon, 8) + 8, 2), :] = pole_send[16 * l + 8 : 16 * l + 10, :]
-
     four = lane >> 2
 
     def packed(tiles):
@@ -213,15 +189,15 @@
             second = jnp.where(four == (g + 1) % groups, z, second)
         return first, second
 
-    def pack_rims(l, carry):
-        at = pl.multiple_of(8 * l, 8)
-        for i, source in enumerate((tr, ka)):
+    def pack_rims(source, target):
+        def one(l, carry):
+            at = pl.multiple_of(8 * l, 8)
             first, second = packed([source[l, PAD + 8 * g : PAD + 8 * g + 8, :] for g in range(groups)])
-            rim_send[0, pl.ds(at + 8 * lev * i, 8), :] = first
-            rim_send[1, pl.ds(at + 8 * lev * i, 8), :] = second
-        return carry
-
-    lax.fori_loop(0, lev, pack_rims, 0)
+            target[0, pl.ds(at, 8), :] = first
+            target[1, pl.ds(at, 8), :] = second
+            return carry
+
+        lax.fori_loop(0, lev, one, 0)
 
     def sideways(src, dst, i):
         return [
@@ -233,10 +209,10 @@
         ]
 
     class Polewards:
-        def __init__(self, step, src, dst, i):
+        def __init__(self, step, src, dst, i, aside=0):
             self.copy = lambda: pltpu.make_async_remote_copy(
                 src_ref=src, dst_ref=dst, send_sem=x_ss.at[i], recv_sem=x_rs.at[i],
-                device_id=(band(step), lon), device_id_type=MESH,
+                device_id=(band(step), sector(aside)), device_id_type=MESH,
             )
             self.sends = lat < bands - 1 if step == 1 else lat > 0
             self.takes = lat > 0 if step == 1 else lat < bands - 1
@@ -262,8 +238,44 @@
             Polewards(-1, ref.at[:, pl.ds(PAD, 8), :], ref.at[:, pl.ds(PAD + rows, 8), :], i + 1),
         ]
 
-    x0 = sideways(rim_send, rim_recv, 0) + over_rows(tr, 2) + over_rows(ka, 4)
+    def diagonal(src, dst, i):
+        return [
+            Polewards(step, src.at[j], dst.at[2 * s + j], i + 2 * s + j, 1 - 2 * j)
+            for s, step in enumerate((1, -1))
+            for j in range(2)
+        ]
+
+    pack_rims(tr, rim_send)
+    x0 = sideways(rim_send, rim_recv, 0) + over_rows(tr, 2)
     for copy in x0:
+        copy.start()
+
+    loads[3].wait()
+    for l in range(lev):
+        pole_send[16 * l : 16 * l + 8, :] = ka[l, pl.ds(tip_tile + PAD, 8), :]
+        pole_send[16 * l + 8 : 16 * l + 9, :] = tr[l, pl.ds(tip + PAD, 1), :]
+        pole_send[16 * l + 9 : 16 * l + 10, :] = wn[l, pl.ds(tip, 1), :]
+
+    def pole_copy(l):
+        return pltpu.make_async_remote_copy(
+            src_ref=pole_send.at[pl.ds(16 * l, 10), :], dst_ref=pole_recv.at[pl.ds(pl.multiple_of(16 * lon, 8), 10), :],
+            send_sem=b_ss.at[l], recv_sem=b_rs.at[lon],
+            device_id=(lat, l * slices + tip_slice), device_id_type=MESH,
+        )
+
+    for l in range(lev):
+        @pl.when(lon != l * slices + tip_slice)
+        def _(l=l):
+            pole_copy(l).start()
+
+        @pl.when(lon == l * slices + tip_slice)
+        def _(l=l):
+            pole_recv[pl.ds(pl.multiple_of(16 * lon, 8), 8), :] = pole_send[16 * l : 16 * l + 8, :]
+            pole_recv[pl.ds(pl.multiple_of(16 * lon, 8) + 8, 2), :] = pole_send[16 * l + 8 : 16 * l + 10, :]
+
+    pack_rims(ka, kap_send)
+    xk = sideways(kap_send, kap_recv, 4) + over_rows(ka, 6) + diagonal(kap_send, kap_diag, 8)
+    for copy in xk:
         copy.start()
     for load in loads[4:]:
         load.wait()
@@ -297,7 +309,6 @@
             turn = wn[l, 8 * g : 8 * g + 8, :] * (tr[l, at + 1 : at + 9, :] - tr[l, at - 1 : at + 7, :])
             value = x - COURANT * 0.5 * (we[l, 8 * g : 8 * g + 8, :] * (e - w) + turn)
             field[l, at : at + 8, :] = value
-            filtered[l, 8 * g : 8 * g + 8, :] = value
             k = ka[l, at : at + 8, :]
             inverse = 1.0 / (1.0 + 4.0 * k)
             invert[l, at : at + 8, :] = inverse
@@ -308,11 +319,6 @@
         at = pl.multiple_of(8 * l, 8)
         adv_send[0, pl.ds(at, 8), :] = first
         adv_send[1, pl.ds(at, 8), :] = second
-        for at in (PAD - 8, PAD + rows):
-            k = ka[l, at : at + 8, :]
-            inverse = 1.0 / (1.0 + 4.0 * k)
-            invert[l, at : at + 8, :] = inverse
-            coupling[l, at : at + 8, :] = k * inverse
         return carry
 
     lax.fori_loop(0, lev, renew, 0)
@@ -324,20 +330,7 @@
             near_east = jnp.where(mine, send[0, at : at + 8, :], recv[1, at : at + 8, :])
             put(kk, jnp.where((lane & 15) < 8, roll(near_west, -4 * kk), roll(near_east, 8 - 4 * kk)))
 
-    for l in range(lev):
-        def put(kk, tile, l=l):
-            side_kappa[l, 12 + 8 * kk : 20 + 8 * kk, :] = tile
-            if kk == 3:
-                kcorner_send[0, 8 * l : 8 * l + 8, :] = tile
-            if kk == 0:
-                kcorner_send[1, 8 * l : 8 * l + 8, :] = tile
-
-        sided(rim_send, rim_recv, 8 * (lev + l), put)
-
-    def corners(send, recv, i):
-        return [Polewards(1, send.at[0], recv.at[0], i), Polewards(-1, send.at[1], recv.at[1], i + 1)]
-
-    x1 = sideways(adv_send, adv_recv, 6) + over_rows(field, 8) + corners(kcorner_send, kcorner_recv, 10)
+    x1 = sideways(adv_send, adv_recv, 12) + over_rows(field, 14) + diagonal(adv_send, adv_diag, 16)
     for copy in x1:
         copy.start()
 
@@ -375,16 +368,16 @@
     for copy in a_copies:
         copy.wait_recv()
 
-    def rows_of(ref):
+    def rows_of(ref, at):
         return [
             jnp.concatenate(
-                [ref[(8 * h + k) * DEEP + share : (8 * h + k) * DEEP + share + 1, :] for k in range(8)], axis=0
+                [ref[(8 * h + k) * DEEP + at : (8 * h + k) * DEEP + at + 1, :] for k in range(8)], axis=0
             )
             for h in range(2)
         ]
 
     fixes = []
-    for v in swapped(*rows_of(recv_a)):
+    for v in swapped(*rows_of(recv_a, share)):
         fixes.append(COURANT * 0.5 * v * jnp.where(eight == 6, roll(v, 11), -roll(v, -7)))
     at_tip = [(row8 == 0) & north & keeper, (row8 == 7) & last & keeper]
     ends = (lane == 0) | (lane == width - 1)
@@ -442,16 +435,19 @@
         send_d[d * DEEP : d * DEEP + share, :] = smooth[d]
         for h in range(2):
             edges[h] = jnp.where((lane >> 3) == d, roll(smooth[d][8 * h : 8 * h + 8], 8 * d + 4), edges[h])
-    edges = [jnp.where(eight < 4, roll(v, 8), roll(v, -8)) for v in edges]
-    for h, v in enumerate(swapped(*edges)):
-        for k in range(8):
-            send_d[(8 * h + k) * DEEP + share : (8 * h + k) * DEEP + share + 1, :] = v[k : k + 1]
-
-    d_copies = across(send_d, recv_d, DEEP, share + 1, d_ss, d_rs)
+    beyond = [jnp.where(eight < 4, roll(v, 8), roll(v, -8)) for v in edges]
+    for i in range(2):
+        west, east = (beyond, edges) if i == 0 else (edges, beyond)
+        for h, v in enumerate(swapped(*[jnp.where(eight < 4, w, e) for w, e in zip(west, east)])):
+            for k in range(8):
+                at = (8 * h + k) * DEEP + share + i
+                send_d[at : at + 1, :] = v[k : k + 1]
+
+    d_copies = across(send_d, recv_d, DEEP, share + 2, d_ss, d_rs)
     for copy in d_copies:
         copy.start()
     recv_d[pl.ds(own, share), :] = send_d[pl.ds(own, share), :]
-    recv_d[pl.ds(own + share, 1), :] = send_d[pl.ds(own + share, 1), :]
+    recv_d[pl.ds(own + share, 2), :] = send_d[pl.ds(own + share, 2), :]
 
     me = lax.div(lon, slices)
 
@@ -499,40 +495,56 @@
                 cross_copy(d).start()
         cross_recv[pl.ds(pl.multiple_of(8 * me, 8), 5), :] = cross_send[pl.ds(pl.multiple_of(8 * lon, 8), 5), :]
 
+    for copy in xk:
+        copy.wait_recv()
+
+    def corners(ref, diag, l):
+        top, bottom = ref[l, PAD - 8 : PAD, :], ref[l, PAD + rows : PAD + rows + 8, :]
+        nw, ne, sw, se = [diag[i, 8 * l : 8 * l + 8, :] for i in range(4)]
+        first = jnp.where(
+            lane < 8, roll(jnp.where(lane >= width - 4, nw, top), 4), roll(jnp.where(lane < 4, ne, top), 12)
+        )
+        second = jnp.where(
+            lane < width - 8,
+            jnp.where(lane < width - 12, roll(sw, -16), roll(bottom, -12)),
+            jnp.where(lane < width - 4, roll(bottom, -4), roll(se, -8)),
+        )
+        return first, second
+
+    def capped(first_tile, last_tile, first, second):
+        return jnp.where(lane < 16, first, roll(last_tile, 16)), jnp.where(lane >= width - 16, second, roll(first_tile, -16))
+
+    for l in range(lev):
+        tiles = []
+
+        def put(kk, tile, l=l, tiles=tiles):
+            side_invert[l, 12 + 8 * kk : 20 + 8 * kk, :] = tile
+            tiles.append(tile)
+
+        sided(kap_send, kap_recv, 8 * l, put)
+        top, bottom = capped(tiles[0], tiles[3], *corners(ka, kap_diag, l))
+        side_invert[l, 4:12, :] = top
+        side_invert[l, 44:52, :] = bottom
+        for j in range(5):
+            at = 8 + 8 * j
+            k = side_invert[l, at : at + 8, :]
+            inverse = 1.0 / (1.0 + 4.0 * k)
+            side_invert[l, at : at + 8, :] = inverse
+            side_coupling[l, at : at + 8, :] = k * inverse
     for copy in x1:
         copy.wait_recv()
     for l in range(lev):
+        for at in (PAD - 8, PAD + rows):
+            k = ka[l, at : at + 8, :]
+            inverse = 1.0 / (1.0 + 4.0 * k)
+            coupling[l, at : at + 8, :] = k * inverse
+            scaled[l, at : at + 8, :] = field[l, at : at + 8, :] * inverse
+
         def put(kk, tile, l=l):
             side_tiles[32 * l + 8 * kk : 32 * l + 8 * kk + 8, :] = tile
-            if kk == 3:
-                corner_send[0, 8 * l : 8 * l + 8, :] = tile
-            if kk == 0:
-                corner_send[1, 8 * l : 8 * l + 8, :] = tile
 
         sided(adv_send, adv_recv, 8 * l, put)
-    x2 = corners(corner_send, corner_recv, 12)
-    for copy in x2:
-        copy.start()
-
-    def capped(first_tile, last_tile, recv, l):
-        top = roll(jnp.where(lane < width - 16, last_tile, recv[0, 8 * l : 8 * l + 8, :]), 16)
-        bottom = roll(jnp.where(lane >= 16, first_tile, recv[1, 8 * l : 8 * l + 8, :]), -16)
-        return top, bottom
-
-    for l in range(lev):
-        top, bottom = capped(kcorner_send[1, 8 * l : 8 * l + 8, :], kcorner_send[0, 8 * l : 8 * l + 8, :], kcorner_recv, l)
-        side_kappa[l, 4:12, :] = top
-        side_kappa[l, 44:52, :] = bottom
-        for j in range(5):
-            at = 8 + 8 * j
-            k = side_kappa[l, at : at + 8, :]
-            inverse = 1.0 / (1.0 + 4.0 * k)
-            side_kappa[l, at : at + 8, :] = inverse
-            side_coupling[l, at : at + 8, :] = k * inverse
-        for at in (PAD - 8, PAD + rows):
-            scaled[l, at : at + 8, :] = field[l, at : at + 8, :] * invert[l, at : at + 8, :]
-    for copy in x2:
-        copy.wait_recv()
+        corner[0, 8 * l : 8 * l + 8, :], corner[1, 8 * l : 8 * l + 8, :] = corners(field, adv_diag, l)
 
     for copy in d_copies:
         copy.wait_recv()
@@ -552,20 +564,16 @@
             at = base + PAD + q * share
             field[l, pl.ds(at, share), :] = x
             scaled[l, pl.ds(at, share), :] = x * invert[l, pl.ds(at, share), :]
-            filtered[l, pl.ds(base + q * share, share), :] = x
-
-    def set_cross(target, t):
-        @pl.when(north)
-        def _():
-            for l in range(lev):
-                target[l, PAD - 1 : PAD, :] = cross_recv[8 * l + t : 8 * l + t + 1, :]
-
-        @pl.when(last)
-        def _():
-            for l in range(lev):
-                target[l, PAD + rows : PAD + rows + 1, :] = cross_recv[8 * l + t : 8 * l + t + 1, :]
-
-    set_cross(field, 0)
+
+    @pl.when(north)
+    def _():
+        for l in range(lev):
+            field[l, PAD - 1 : PAD, :] = cross_recv[8 * l : 8 * l + 1, :]
+
+    @pl.when(last)
+    def _():
+        for l in range(lev):
+            field[l, PAD + rows : PAD + rows + 1, :] = cross_recv[8 * l : 8 * l + 1, :]
 
     halo = jnp.concatenate([cross_recv[8 * l + 4 : 8 * l + 5, :] for l in range(lev)] * 2, axis=0)
     for t in range(SWEEPS):
@@ -575,9 +583,12 @@
             jnp.where(lane < 4, roll(halo, -8 * t), roll(plain, 4)),
             jnp.where(lane < 12, roll(plain, 12), roll(halo, 8 - 8 * t)),
         )
-        side_cross[t] = jnp.where(last, roll(z, -16), z)
-
-    outside = [jnp.where(last, roll(v, 96), v) for v in swapped(*rows_of(recv_d))]
+        side_cross[t, :8, :] = jnp.where(last, roll(z, -16), z)
+        side_cross[t, 8:, :] = plain
+
+    strips = [
+        [jnp.where(last, roll(v, -32), v) for v in swapped(*rows_of(recv_d, share + i))] for i in range(2)
+    ]
     from_cap = jnp.where(last, lane - (width - 32), lane)
     inside_cap = polar & (from_cap >= 0) & (from_cap < 32)
     top_spot = north & (row8 == 7) & (lane < 16)
@@ -585,69 +596,20 @@
     for l in range(lev):
         tiles = []
         for kk in range(4):
-            z = zero
-            for g in range(2):
-                k, h = l * slices + 2 * g + kk // 2, kk % 2
-                x = recv_d[k * DEEP + 8 * h : k * DEEP + 8 * h + 8, :]
-                part = lane - 16 * g
-                inner = jnp.where(part < 8, roll(x, 16 * g + 4), roll(x, 16 * g + 12))
-                inner = jnp.where(last, roll(inner, 96), inner)
-                z_outer = outside[h]
-                here = from_cap - 16 * g
-                outer = jnp.where(here < 8, roll(z_outer, 16 * g - 8 * k), roll(z_outer, 16 * g + 8 - 8 * k))
-                value = jnp.where((here >= 4) & (here < 12), inner, outer)
-                z = jnp.where((here >= 0) & (here < 16), value, z)
+            h, by = kk % 2, -32 * l - 8 * (kk // 2)
+            z = jnp.where((lane & 15) < 8, roll(strips[0][h], by), roll(strips[1][h], by + 8))
             tile = jnp.where(inside_cap, z, side_tiles[32 * l + 8 * kk : 32 * l + 8 * kk + 8, :])
-            side[0, l, 12 + 8 * kk : 20 + 8 * kk, :] = tile
+            side[l, 12 + 8 * kk : 20 + 8 * kk, :] = tile
             tiles.append(tile)
-        top, bottom = capped(tiles[0], tiles[3], corner_recv, l)
-        side[0, l, 4:12, :] = jnp.where(top_spot, side_cross[0, l : l + 1, :], top)
-        side[0, l, 44:52, :] = jnp.where(bottom_spot, side_cross[0, l : l + 1, :], bottom)
-
-    for t in range(SWEEPS - 1):
-        for l in range(lev):
-            for j in range(5):
-                at = 8 + 8 * j
-                x = side[t, l, at : at + 8, :]
-                total = roll(x, 1) + roll(x, -1) + side[t, l, at - 1 : at + 7, :] + side[t, l, at + 1 : at + 9, :]
-                if t == 0:
-                    source = x * side_kappa[l, at : at + 8, :]
-                    side_scaled[l, at : at + 8, :] = source
-                else:
-                    source = side_scaled[l, at : at + 8, :]
-                x = source + side_coupling[l, at : at + 8, :] * total
-                if j == 0:
-                    x = jnp.where(north & (row8 == 3) & (lane < 16), side_cross[t + 1, l : l + 1, :], x)
-                if j == 4:
-                    x = jnp.where(last & (row8 == 4) & (lane >= width - 16), side_cross[t + 1, l : l + 1, :], x)
-                side[t + 1, l, at : at + 8, :] = x
-
-    chain = [field, ping, pong, ping, balanced]
-    for sweep in range(SWEEPS):
-        source, target = chain[sweep], chain[sweep + 1]
-        final = sweep == SWEEPS - 1
-
-        def relax(l, carry, sweep=sweep, source=source, target=target, final=final):
-            for kk in range(4) if final else range(-1, 5):
-                h = side[sweep, l, 12 + 8 * kk : 20 + 8 * kk, :]
-                h = jnp.where((lane & 15) == 3, h, roll(h, -10))
-                for g in range(groups // 4) if 0 <= kk < 4 else ((0,) if kk < 0 else (groups // 4 - 1,)):
-                    at = PAD + 32 * g + 8 * kk
-                    edge = roll(h, -(16 * g + 3))
-                    x = source[l, at : at + 8, :]
-                    w = jnp.where(lane == 0, edge, roll(x, 1))
-                    e = jnp.where(lane == width - 1, edge, roll(x, -1))
-                    total = (w + e) + (source[l, at - 1 : at + 7, :] + source[l, at + 1 : at + 9, :])
-                    value = scaled[l, at : at + 8, :] + coupling[l, at : at + 8, :] * total
-                    put = at - PAD if final else at
-                    target[l, put : put + 8, :] = value
-            return carry
-
-        lax.fori_loop(0, lev, relax, 0)
-        if not final:
-            set_cross(target, sweep + 1)
-
-    for copy in a_copies + x0 + x1 + d_copies + x2:
+        at = 8 * l
+        top, bottom = capped(tiles[0], tiles[3], corner[0, at : at + 8, :], corner[1, at : at + 8, :])
+        side[l, 4:12, :] = jnp.where(top_spot, side_cross[0, l : l + 1, :], top)
+        side[l, 44:52, :] = jnp.where(bottom_spot, side_cross[0, l : l + 1, :], bottom)
+        for j in range(5):
+            at = 8 + 8 * j
+            side_scaled[l, at : at + 8, :] = side[l, at : at + 8, :] * side_invert[l, at : at + 8, :]
+
+    for copy in a_copies + x0 + xk + x1 + d_copies:
         copy.wait_send()
     for l in range(lev):
         @pl.when(lon != l * slices + tip_slice)
@@ -662,49 +624,148 @@
                 cross_copy(d).wait_send()
 
 
+def relax(
+    bands, field, scaled, coupling, side0, side_scaled, side_coupling, side_cross, filtered, balanced, stack, side, sems
+):
+    lev, rows, width = filtered.shape
+    groups = rows // 8
+    bf16, f32 = jnp.bfloat16, jnp.float32
+    lat = lax.axis_index("lat")
+    north, last = lat == 0, lat == bands - 1
+    out = pltpu.make_async_copy(field.at[:, pl.ds(PAD, rows), :], filtered, sems.at[0])
+    out.start()
+    lane = lax.broadcasted_iota(jnp.int32, (8, width), 1)
+    row8 = lax.broadcasted_iota(jnp.int32, (8, width), 0)
+    at16 = lane & 15
+    one = lax.broadcasted_iota(jnp.int32, (width, width), 0)
+    two = lax.broadcasted_iota(jnp.int32, (width, width), 1)
+    shift = jnp.where((one - two == 1) | (two - one == 1), 1.0, 0.0).astype(bf16)
+    spot = one & 15
+    from_west = (two == 0) & ((spot == 3) | (spot == 4))
+    from_east = (two == width - 1) & ((spot == 12) | (spot == 13))
+    weights = jnp.concatenate([shift, shift, jnp.where(from_west | from_east, 1.0, 0.0).astype(bf16)], axis=0)
+
+    def roll(x, by):
+        return pltpu.roll(x, by % width, 1)
+
+    def parts(x):
+        high = x.astype(bf16)
+        return high, (x - high.astype(f32)).astype(bf16)
+
+    def level(source, target, beside, l):
+        ends = {}
+        for kk in range(-1, 5):
+            high, low = parts(beside(l, 12 + 8 * kk))
+            ends[kk] = jnp.where(
+                (at16 == 3) | (at16 == 12), high.astype(f32),
+                jnp.where((at16 == 4) | (at16 == 13), roll(low.astype(f32), 1), 0.0),
+            )
+        order = [(0, -1)] + [(i // 4, i % 4) for i in range(groups)] + [(groups // 4 - 1, 4)]
+        high, low = parts(source(l, PAD - 8, rows + 16))
+        edge = jnp.concatenate([jnp.where((lane >> 4) == g, ends[kk], 0.0) for g, kk in order], axis=0).astype(bf16)
+        total = jnp.dot(jnp.concatenate([high, low, edge], axis=1), weights, preferred_element_type=f32)
+        for i in range(groups + 2):
+            at = PAD - 8 + 8 * i
+            value = total[8 * i : 8 * i + 8] + (source(l, at - 1, 8) + source(l, at + 1, 8))
+            target(l, at, scaled[l, at : at + 8, :] + coupling[l, at : at + 8, :] * value)
+
+    for l in range(lev):
+        stack[0, l, PAD - 16 : PAD + rows + 16, :] = field[l]
+        side[0, l] = side0[l]
+
+    def sweep(t, carry):
+        def source(l, at, count):
+            return stack[t, l, at : at + count, :]
+
+        def target(l, at, value):
+            stack[t + 1, l, at : at + 8, :] = value
+
+        def beside(l, at):
+            return side[t, l, at : at + 8, :]
+
+        for l in range(lev):
+            level(source, target, beside, l)
+            for j in range(5):
+                at = 8 + 8 * j
+                x = beside(l, at)
+                total = roll(x, 1) + roll(x, -1) + beside(l, at - 1) + beside(l, at + 1)
+                x = side_scaled[l, at : at + 8, :] + side_coupling[l, at : at + 8, :] * total
+                cross = side_cross[t + 1, pl.ds(l, 1), :]
+                if j == 0:
+                    x = jnp.where(north & (row8 == 3) & (lane < 16), cross, x)
+                if j == 4:
+                    x = jnp.where(last & (row8 == 4) & (lane >= width - 16), cross, x)
+                side[t + 1, l, at : at + 8, :] = x
+        for l in range(lev):
+            cross = side_cross[t + 1, pl.ds(8 + l, 1), :]
+            for here, at in ((north, PAD - 1), (last, PAD + rows)):
+                stack[t + 1, l, at : at + 1, :] = jnp.where(here, cross, stack[t + 1, l, at : at + 1, :])
+        return carry
+
+    lax.fori_loop(0, SWEEPS - 1, sweep, 0)
+    copies = [out]
+    for l in range(lev):
+        level(
+            lambda l, at, count: stack[SWEEPS - 1, l, at : at + count, :],
+            lambda l, at, value: stack.__setitem__((SWEEPS, l, slice(at, at + 8), slice(None)), value),
+            lambda l, at: side[SWEEPS - 1, l, at : at + 8, :],
+            l,
+        )
+        copy = pltpu.make_async_copy(stack.at[SWEEPS, l, pl.ds(PAD, rows), :], balanced.at[l], sems.at[1 + l])
+        copy.start()
+        copies.append(copy)
+    for copy in copies:
+        copy.wait()
+
+
 def solution(mesh):
     sectors, bands = mesh.shape["lon"], mesh.shape["lat"]
 
     def per_device(tracer, wind_east, wind_north, kappa, cutoff, partner):
         lev, rows, width = tracer.shape
         f32 = jnp.float32
-        block = pltpu.VMEM((lev, rows, width), f32)
-        tall = pltpu.VMEM((lev, rows + 2 * PAD, width), f32)
-        strips = pltpu.VMEM((sectors * DEEP, width), f32)
-        pair = pltpu.VMEM((2, lev * 8, width), f32)
-        narrow = pltpu.VMEM((lev, 56, width), f32)
+        high = rows + 2 * PAD
+
+        def array(*shape):
+            return pltpu.VMEM(shape, f32)
+
+        block, tall = array(lev, rows, width), array(lev, high, width)
+        strips = array(sectors * DEEP, width)
+        pair, four = array(2, lev * 8, width), array(4, lev * 8, width)
+        narrow = array(lev, 56, width)
         vmem = pl.BlockSpec(memory_space=pltpu.VMEM)
+        hbm = pl.BlockSpec(memory_space=pltpu.HBM)
         small = (cutoff.reshape(1, -1), partner.reshape(sectors, width), *tables(sectors, width))
         dma = pltpu.SemaphoreType.DMA
-        return pl.pallas_call(
+        made = [(lev, high, width)] * 3 + [(lev, 56, width)] * 3 + [(SWEEPS, 16, width)]
+        limit = 24 * 1024 * 1024
+        held = pl.pallas_call(
             functools.partial(kernel, sectors, bands),
-            out_shape=[jax.ShapeDtypeStruct(tracer.shape, f32)] * 2,
-            in_specs=[pl.BlockSpec(memory_space=pltpu.HBM)] * 10,
-            out_specs=[vmem] * 2,
+            out_shape=[jax.ShapeDtypeStruct(shape, f32) for shape in made],
+            in_specs=[hbm] * 10,
+            out_specs=[vmem] * len(made),
             scratch_shapes=[
                 tall, block, block, tall,
-                pltpu.VMEM((1, cutoff.shape[0]), jnp.int32), pltpu.VMEM((sectors, width), jnp.int32),
-                *[pltpu.VMEM(a.shape, a.dtype) for a in small[2:]],
+                *[pltpu.VMEM(a.shape, a.dtype) for a in small],
                 dma((10,)),
-                strips, strips,
-                pltpu.VMEM((16 * lev, width), f32), pltpu.VMEM((16 * sectors, width), f32),
-                strips, strips,
-                pltpu.VMEM((8 * sectors, width), f32), pltpu.VMEM((8 * lev, width), f32),
-                pltpu.VMEM((sectors, width), f32), pltpu.VMEM((8 * sectors, width), f32),
-                pltpu.VMEM((2, 2 * lev * 8, width), f32), pltpu.VMEM((2, 2 * lev * 8, width), f32),
-                pair, pair, pair, pair, pair, pair,
-                tall, tall, tall, tall, tall, tall,
-                pltpu.VMEM((lev * 32, width), f32), pltpu.VMEM((SWEEPS, lev, 56, width), f32),
-                narrow, narrow, narrow, pltpu.VMEM((SWEEPS, 8, width), f32),
+                strips, strips, array(16 * lev, width), array(16 * sectors, width), strips, strips,
+                array(8 * sectors, width), array(8 * lev, width), array(sectors, width),
+                pair, pair, pair, pair, four, pair, pair, four, pair, tall, array(lev * 32, width), narrow,
                 *[dma((sectors,))] * 4,
-                dma((lev,)), dma((sectors,)), dma((sectors,)), dma((lev,)), dma((14,)), dma((14,)),
+                dma((lev,)), dma((sectors,)), dma((sectors,)), dma((lev,)), dma((20,)), dma((20,)),
             ],
-            compiler_params=pltpu.CompilerParams(
-                collective_id=0, has_side_effects=True, vmem_limit_bytes=32 * 1024 * 1024
-            ),
+            compiler_params=pltpu.CompilerParams(collective_id=0, has_side_effects=True, vmem_limit_bytes=limit),
         )(
             *[pltpu.with_memory_space_constraint(jnp.asarray(a), pltpu.HBM) for a in (tracer, wind_east, wind_north, kappa, *small)]
         )
+        return pl.pallas_call(
+            functools.partial(relax, bands),
+            out_shape=[jax.ShapeDtypeStruct(tracer.shape, f32)] * 2,
+            in_specs=[vmem] * len(made),
+            out_specs=[hbm] * 2,
+            scratch_shapes=[array(SWEEPS + 1, lev, high, width), array(SWEEPS, lev, 56, width), dma((1 + lev,))],
+            compiler_params=pltpu.CompilerParams(vmem_limit_bytes=limit),
+        )(*[pltpu.with_memory_space_constraint(a, pltpu.VMEM) for a in held])
 
     spec = P(None, "lat", "lon")
     return jax.shard_map(

time: 28.5 us -> 24.1 us (0.85)
  Pallas kernels: 26.1 us -> 23.3 us
  local copies, waits for them, and re-layouts: 1.59 us -> 0 us
    pallas_call x1, Pallas kernels: 26.1 us -> 20.5 us  [per_device(): pl.pallas_call(functools.partial(kernel, sectors, bands), out_shape=[jax....]
    pallas_call x0 -> x1, Pallas kernels: none -> 2.79 us  [per_device(): pl.pallas_call(functools.partial(relax, bands), out_shape=[jax.ShapeDtype...]
    unnamed x2 -> x0, local copies, waits for them, and re-layouts: 1.59 us -> none
where the time goes in v2:
time: 24.1 us; the launch traced here: 24 us
  Pallas kernels  23.3 us (97%)
  between operations  0.64 us (3%)
    pallas_call x1, Pallas kernels, per_device(): pl.pallas_call(functools.partial(kernel, sectors, bands), out_shape=[jax....  20.5 us
    pallas_call x1, Pallas kernels, per_device(): pl.pallas_call(functools.partial(relax, bands), out_shape=[jax.ShapeDtype...  2.79 us

profile of v2, /device:TPU:0, one launch (start us, length us, event | category | flops | bytes accessed | tf_op | source)
XLA Modules:
  0.0 24.0 jit_solution(15329080955224273415)
XLA Ops:
  0.6 20.5 %shard_map.113 = (f32[4,288,128]{2,1,0:T(8,128)S(1)}, f32[4,288,128]{2,1,0:T(8,128)S(1)}, f32[4,288,128]{2,1,0:T(8,128)S(1)}, f32[4,56,128]{2,1,0:T(8,128)S(1)},...) custom-call(f32[4,256,128]{2,1,0:T(8,128)} %tracer_h.1, ...), custom_call_target="tpu_custom_call" | custom-call | tf_op jit(solution)/shard_map/pallas_call | solution.py:742
  21.2 2.8 %shard_map.114 = (f32[4,256,128]{2,1,0:T(8,128)}, f32[4,256,128]{2,1,0:T(8,128)}) custom-call(f32[4,288,128]{2,1,0:T(8,128)S(1)} %get-tuple-element.9.field, f32[4,288,128]{2,1,0:T(8,128)S(1)} %get-tuple-element.10.scaled, f32[4,288,128]{2,1,0:T(8,128)S(1)} %get-tuple-element.11.coupling, f32[4,56,128]{2,1,0:T(8,128)S(1)} %get-tuple-element.12.side0, ...), custom_call_target="tpu_custom_call" | custom-call | tf_op jit(solution)/shard_map/pallas_call | solution.py:761

commit v3 on v2

--- a/solution.py
+++ b/solution.py
@@ -48,16 +48,47 @@
     return jnp.take_along_axis(x, at_lane, axis=1, mode="promise_in_bounds")
 
 
+def parts(x):
+    high = x.astype(jnp.bfloat16)
+    return high, (x - high.astype(jnp.float32)).astype(jnp.bfloat16)
+
+
+def shift_weights(width):
+    one = lax.broadcasted_iota(jnp.int32, (width, width), 0)
+    two = lax.broadcasted_iota(jnp.int32, (width, width), 1)
+    shift = jnp.where((one - two == 1) | (two - one == 1), 1.0, 0.0).astype(jnp.bfloat16)
+    spot = one & 15
+    from_west = (two == 0) & ((spot == 3) | (spot == 4))
+    from_east = (two == width - 1) & ((spot == 12) | (spot == 13))
+    edge = jnp.where(from_west | from_east, 1.0, 0.0).astype(jnp.bfloat16)
+    return jnp.concatenate([shift, shift, edge], axis=0)
+
+
+def rim(h, at16):
+    high, low = parts(h)
+    return jnp.where(
+        (at16 == 3) | (at16 == 12), high.astype(jnp.float32),
+        jnp.where((at16 == 4) | (at16 == 13), pltpu.roll(low.astype(jnp.float32), 1, 1), 0.0),
+    )
+
+
+def west_and_east(x, edges, weights):
+    high, low = parts(x)
+    rims = jnp.concatenate(edges, axis=0).astype(jnp.bfloat16)
+    return jnp.dot(jnp.concatenate([high, low, rims], axis=1), weights, preferred_element_type=jnp.float32)
+
+
 def kernel(
     sectors, bands,
-    tracer_h, wind_east_h, wind_north_h, kappa_h, cutoff_h, partner_h, tw_cos_h, tw_sin_h, fwd_h, inv_h,
-    field, scaled, coupling, side, side_scaled, side_coupling, side_cross,
-    tr, we, wn, ka, cutoff, partner, tw_cos, tw_sin, fwd, inv, load_s,
-    send_a, recv_a, pole_send, pole_recv, send_d, recv_d, cross_send, cross_recv, beyond_fix,
-    rim_send, rim_recv, kap_send, kap_recv, kap_diag, adv_send, adv_recv, adv_diag, corner, invert, side_tiles, side_invert,
-    a_ss, a_rs, d_ss, d_rs, b_ss, b_rs, c_ss, c_rs, x_ss, x_rs,
+    tracer_h, wind_east_h, wind_north_h, kappa_h, cutoff_h, partner_h, table_h,
+    stack, scaled, coupling, side, side_scaled, side_coupling, side_cross,
+    tr, we, wn, ka, cutoff, partner, table, load_s,
+    send_a, recv_a, pole_send, pole_recv, send_d, recv_d, beyond_fix,
+    rim_send, rim_recv, kap_send, kap_recv, kap_diag, adv_send, adv_recv, adv_diag, corner, invert, side_tiles, side_invert, early, early_scaled,
+    a_s, a_r, b_s, b_r, d_s, d_r, x_s, x_r, k_s, k_r, f_s, f_r,
 ):
     lev, rows, width = we.shape
+    field = stack.at[0]
     pole = cutoff.shape[1] // 2
     share = lev * pole // sectors
     slices = sectors // lev
@@ -75,6 +106,13 @@
     def band(offset):
         return lax.rem(lat + (offset % bands), bands)
 
+    body = pl.ds(PAD, rows)
+    held = (tracer_h, wind_east_h, wind_north_h, kappa_h, partner_h, cutoff_h, table_h)
+    near = (tr.at[:, body, :], we, wn, ka.at[:, body, :], partner, cutoff, table)
+    loads = [pltpu.make_async_copy(h, v, load_s.at[i]) for i, (h, v) in enumerate(zip(held, near))]
+    for load in loads[:3]:
+        load.start()
+
     barrier = pltpu.get_barrier_semaphore()
     for t in range(1, sectors):
         pl.semaphore_signal(barrier, inc=1, device_id=(lat, sector(t)), device_id_type=MESH)
@@ -83,11 +121,7 @@
         for i in (-1, 0, 1):
             pl.semaphore_signal(barrier, inc=1, device_id=(band(t), sector(i)), device_id_type=MESH)
 
-    body = pl.ds(PAD, rows)
-    held = (tracer_h, wind_east_h, wind_north_h, kappa_h, partner_h, cutoff_h, tw_cos_h, tw_sin_h, fwd_h, inv_h)
-    near = (tr.at[:, body, :], we, wn, ka.at[:, body, :], partner, cutoff, tw_cos, tw_sin, fwd, inv)
-    loads = [pltpu.make_async_copy(h, v, load_s.at[i]) for i, (h, v) in enumerate(zip(held, near))]
-    for load in loads:
+    for load in loads[3:]:
         load.start()
 
     lane = lax.broadcasted_iota(jnp.int32, (8, width), 1)
@@ -158,26 +192,35 @@
                 )
                 packs[h] = jnp.where((lane >> 3) == k, t, packs[h])
     for h, v in enumerate(swapped(*packs)):
-        for k in range(8):
-            send_a[(8 * h + k) * DEEP + share : (8 * h + k) * DEEP + share + 1, :] = v[k : k + 1]
+        send_a[pl.ds(8 * h * DEEP + share, 8, stride=DEEP), :] = v
 
     pl.semaphore_wait(barrier, sectors - 1 + 3 * len(beside))
 
-    def across(src, dst, stride, count, ss, rs):
-        copies = []
+    def across(src, dst, count, ss, rs):
         for t in range(1, sectors):
-            copies.append(
-                pltpu.make_async_remote_copy(
-                    src_ref=src.at[pl.ds(pl.multiple_of(sector(t) * stride, 8), count), :],
-                    dst_ref=dst.at[pl.ds(pl.multiple_of(lon * stride, 8), count), :],
-                    send_sem=ss.at[t], recv_sem=rs.at[t], device_id=(lat, sector(t)), device_id_type=MESH,
-                )
-            )
-        return copies
-
-    a_copies = across(send_a, recv_a, DEEP, share + 1, a_ss, a_rs)
-    for copy in a_copies:
-        copy.start()
+            there = sector(t)
+            pltpu.make_async_remote_copy(
+                src_ref=src.at[pl.ds(pl.multiple_of(there * DEEP, 8), count), :],
+                dst_ref=dst.at[pl.ds(pl.multiple_of(lon * DEEP, 8), count), :],
+                send_sem=ss, recv_sem=rs, device_id=(lat, there), device_id_type=MESH,
+            ).start()
+
+    def bulk(count, sem):
+        whole = send_d.at[pl.ds(0, count), :]
+        return pltpu.make_async_remote_copy(
+            src_ref=whole, dst_ref=whole, send_sem=sem, recv_sem=sem, device_id=(lat, sector(1)), device_id_type=MESH
+        )
+
+    def split_wait(single, double, sem, send):
+        for here, count in ((polar, single), (jnp.logical_not(polar), double)):
+            @pl.when(here)
+            def _(count=count):
+                if send:
+                    bulk(count, sem).wait_send()
+                else:
+                    bulk(count, sem).wait_recv()
+
+    across(send_a, recv_a, share + 1, a_s, a_r)
 
     four = lane >> 2
 
@@ -199,56 +242,36 @@
 
         lax.fori_loop(0, lev, one, 0)
 
-    def sideways(src, dst, i):
-        return [
+    def sideways(src, dst, ss, rs):
+        for j in range(2):
             pltpu.make_async_remote_copy(
-                src_ref=src.at[j], dst_ref=dst.at[j], send_sem=x_ss.at[i + j], recv_sem=x_rs.at[i + j],
+                src_ref=src.at[j], dst_ref=dst.at[j], send_sem=ss, recv_sem=rs,
                 device_id=(lat, sector(1 - 2 * j)), device_id_type=MESH,
-            )
-            for j in range(2)
-        ]
-
-    class Polewards:
-        def __init__(self, step, src, dst, i, aside=0):
-            self.copy = lambda: pltpu.make_async_remote_copy(
-                src_ref=src, dst_ref=dst, send_sem=x_ss.at[i], recv_sem=x_rs.at[i],
-                device_id=(band(step), sector(aside)), device_id_type=MESH,
-            )
-            self.sends = lat < bands - 1 if step == 1 else lat > 0
-            self.takes = lat > 0 if step == 1 else lat < bands - 1
-
-        def start(self):
-            @pl.when(self.sends)
-            def _():
-                self.copy().start()
-
-        def wait_recv(self):
-            @pl.when(self.takes)
-            def _():
-                self.copy().wait_recv()
-
-        def wait_send(self):
-            @pl.when(self.sends)
-            def _():
-                self.copy().wait_send()
-
-    def over_rows(ref, i):
-        return [
-            Polewards(1, ref.at[:, pl.ds(PAD + rows - 8, 8), :], ref.at[:, pl.ds(PAD - 8, 8), :], i),
-            Polewards(-1, ref.at[:, pl.ds(PAD, 8), :], ref.at[:, pl.ds(PAD + rows, 8), :], i + 1),
-        ]
-
-    def diagonal(src, dst, i):
-        return [
-            Polewards(step, src.at[j], dst.at[2 * s + j], i + 2 * s + j, 1 - 2 * j)
-            for s, step in enumerate((1, -1))
-            for j in range(2)
-        ]
-
+            ).start()
+
+    def poleward(ref, ss, rs, send=None, recv=None):
+        for i, step in enumerate((1, -1)):
+            plan = [
+                (
+                    ref.at[:, pl.ds(PAD + rows - 8 if step == 1 else PAD, 8), :],
+                    ref.at[:, pl.ds(PAD - 8 if step == 1 else PAD + rows, 8), :], 0,
+                )
+            ]
+            if send is not None:
+                plan += [(send.at[j], recv.at[2 * i + j], 1 - 2 * j) for j in range(2)]
+
+            @pl.when(lat < bands - 1 if step == 1 else lat > 0)
+            def _(step=step, plan=plan):
+                for src, dst, aside in plan:
+                    pltpu.make_async_remote_copy(
+                        src_ref=src, dst_ref=dst, send_sem=ss, recv_sem=rs,
+                        device_id=(band(step), sector(aside)), device_id_type=MESH,
+                    ).start()
+
+    unit = 8 * lev
     pack_rims(tr, rim_send)
-    x0 = sideways(rim_send, rim_recv, 0) + over_rows(tr, 2)
-    for copy in x0:
-        copy.start()
+    sideways(rim_send, rim_recv, x_s, x_r)
+    poleward(tr, x_s, x_r)
 
     loads[3].wait()
     for l in range(lev):
@@ -259,7 +282,7 @@
     def pole_copy(l):
         return pltpu.make_async_remote_copy(
             src_ref=pole_send.at[pl.ds(16 * l, 10), :], dst_ref=pole_recv.at[pl.ds(pl.multiple_of(16 * lon, 8), 10), :],
-            send_sem=b_ss.at[l], recv_sem=b_rs.at[lon],
+            send_sem=b_s, recv_sem=b_r,
             device_id=(lat, l * slices + tip_slice), device_id_type=MESH,
         )
 
@@ -274,9 +297,8 @@
             pole_recv[pl.ds(pl.multiple_of(16 * lon, 8) + 8, 2), :] = pole_send[16 * l + 8 : 16 * l + 10, :]
 
     pack_rims(ka, kap_send)
-    xk = sideways(kap_send, kap_recv, 4) + over_rows(ka, 6) + diagonal(kap_send, kap_diag, 8)
-    for copy in xk:
-        copy.start()
+    sideways(kap_send, kap_recv, k_s, k_r)
+    poleward(ka, k_s, k_r, kap_send, kap_diag)
     for load in loads[4:]:
         load.wait()
 
@@ -291,8 +313,7 @@
             farther, taken(pltpu.roll(points, sectors - half - 1, 0), at_lane), taken(pltpu.roll(points, half, 0), at_lane)
         )
 
-    for copy in x0:
-        copy.wait_recv()
+    split_wait(3 * unit, 4 * unit, x_r, False)
 
     def renew(l, carry):
         at = pl.multiple_of(8 * l, 8)
@@ -330,21 +351,14 @@
             near_east = jnp.where(mine, send[0, at : at + 8, :], recv[1, at : at + 8, :])
             put(kk, jnp.where((lane & 15) < 8, roll(near_west, -4 * kk), roll(near_east, 8 - 4 * kk)))
 
-    x1 = sideways(adv_send, adv_recv, 12) + over_rows(field, 14) + diagonal(adv_send, adv_diag, 16)
-    for copy in x1:
-        copy.start()
+    sideways(adv_send, adv_recv, f_s, f_r)
+    poleward(field, f_s, f_r, adv_send, adv_diag)
 
     beyond_fix[...] = jnp.zeros_like(beyond_fix)
 
     @pl.when(keeper)
     def _():
-        for d in range(sectors):
-            @pl.when(lon != d)
-            def _(d=d):
-                pltpu.make_async_remote_copy(
-                    src_ref=pole_send.at[pl.ds(0, 10), :], dst_ref=pole_recv.at[pl.ds(16 * d, 10), :],
-                    send_sem=b_ss.at[0], recv_sem=b_rs.at[d], device_id=(lat, sector(1)), device_id_type=MESH,
-                ).wait_recv()
+        bulk(10 * (sectors - 1), b_r).wait_recv()
         tips = jnp.concatenate([pole_recv[16 * d + 8 : 16 * d + 9, :] for d in range(sectors)], axis=0)
         winds = jnp.concatenate([pole_recv[16 * d + 9 : 16 * d + 10, :] for d in range(sectors)], axis=0)
         turned = COURANT * 0.5 * winds * crossed(tips)
@@ -365,16 +379,13 @@
     own = pl.multiple_of(lon * DEEP, 8)
     recv_a[pl.ds(own, share), :] = send_a[pl.ds(own, share), :]
     recv_a[pl.ds(own + share, 1), :] = send_a[pl.ds(own + share, 1), :]
-    for copy in a_copies:
-        copy.wait_recv()
+    bulk((share + 1) * (sectors - 1), a_r).wait_recv()
+    tw_cos, tw_sin = table[0 : half + 1, :], table[16 : half + 17, :]
+    fwd = table[32 : 32 + 2 * width, :]
+    inv = jnp.concatenate([table[32 + 2 * width : 32 + 3 * width, :], table[32 + 3 * width : 32 + 4 * width, :]], axis=1)
 
     def rows_of(ref, at):
-        return [
-            jnp.concatenate(
-                [ref[(8 * h + k) * DEEP + at : (8 * h + k) * DEEP + at + 1, :] for k in range(8)], axis=0
-            )
-            for h in range(2)
-        ]
+        return [ref[pl.ds(8 * h * DEEP + at, 8, stride=DEEP), :] for h in range(2)]
 
     fixes = []
     for v in swapped(*rows_of(recv_a, share)):
@@ -406,13 +417,13 @@
         else:
             blocks.append(jnp.concatenate([re * c + im * s, im * c - re * s], axis=1))
     spectrum = jnp.dot(
-        jnp.concatenate(blocks, axis=0), fwd[...], precision=HIGHEST, preferred_element_type=jnp.float32
+        jnp.concatenate(blocks, axis=0), fwd, precision=HIGHEST, preferred_element_type=jnp.float32
     )
     keep = jnp.concatenate(
         [jnp.where(jnp.abs(wave + k).astype(jnp.float32) <= limit, 1.0, 0.0) for k in range(half + 1)], axis=0
     )
     back = jnp.dot(
-        jnp.where(keep > 0.0, spectrum, 0.0), inv[...], precision=HIGHEST, preferred_element_type=jnp.float32
+        jnp.where(keep > 0.0, spectrum, 0.0), inv, precision=HIGHEST, preferred_element_type=jnp.float32
     )
     real, imag = [], []
     for k in range(half + 1):
@@ -439,23 +450,13 @@
     for i in range(2):
         west, east = (beyond, edges) if i == 0 else (edges, beyond)
         for h, v in enumerate(swapped(*[jnp.where(eight < 4, w, e) for w, e in zip(west, east)])):
-            for k in range(8):
-                at = (8 * h + k) * DEEP + share + i
-                send_d[at : at + 1, :] = v[k : k + 1]
-
-    d_copies = across(send_d, recv_d, DEEP, share + 2, d_ss, d_rs)
-    for copy in d_copies:
-        copy.start()
-    recv_d[pl.ds(own, share), :] = send_d[pl.ds(own, share), :]
-    recv_d[pl.ds(own + share, 2), :] = send_d[pl.ds(own + share, 2), :]
-
-    me = lax.div(lon, slices)
-
-    def cross_copy(d):
-        return pltpu.make_async_remote_copy(
-            src_ref=cross_send.at[pl.ds(8 * d, 5), :], dst_ref=cross_recv.at[pl.ds(pl.multiple_of(8 * me, 8), 5), :],
-            send_sem=c_ss.at[d], recv_sem=c_rs.at[me], device_id=(lat, d), device_id_type=MESH,
-        )
+            send_d[pl.ds(8 * h * DEEP + share + i, 8, stride=DEEP), :] = v
+
+    extra = share + 2 + SWEEPS + 1
+
+    def put_cross(t, rows16):
+        for h in range(2):
+            send_d[pl.ds(8 * h * DEEP + share + 2 + t, 8, stride=DEEP), :] = rows16[8 * h : 8 * h + 8]
 
     @pl.when(keeper)
     def _():
@@ -472,8 +473,7 @@
         for t in range(SWEEPS):
             tips = jnp.concatenate([jnp.where(last, x[7:8], x[0:1]) for x in now], axis=0)
             over = crossed(tips)
-            for d in range(sectors):
-                cross_send[8 * d + t : 8 * d + t + 1, :] = over[d : d + 1]
+            put_cross(t, over)
             z = roll(over, 8 * t + 4)
             z = jnp.where((wide & 7) < 4, pltpu.roll(z, 1, 0), pltpu.roll(z, sectors - 1, 0))
             ends = jnp.where((wide >> 3) == t, z, ends)
@@ -487,16 +487,21 @@
                     b = jnp.where((row8 == 7) & last, over[d : d + 1], pltpu.roll(now[d], 7, 0))
                     later.append(source[d] + pull[d] * (w + e + u + b))
                 now = later
-        for d in range(sectors):
-            cross_send[8 * d + 4 : 8 * d + 5, :] = ends[d : d + 1]
-        for d in range(sectors):
-            @pl.when(lon != d)
-            def _(d=d):
-                cross_copy(d).start()
-        cross_recv[pl.ds(pl.multiple_of(8 * me, 8), 5), :] = cross_send[pl.ds(pl.multiple_of(8 * lon, 8), 5), :]
-
-    for copy in xk:
-        copy.wait_recv()
+        put_cross(SWEEPS, ends)
+        across(send_d, recv_d, extra, d_s, d_r)
+
+    @pl.when(jnp.logical_not(keeper))
+    def _():
+        across(send_d, recv_d, share + 2, d_s, d_r)
+
+    recv_d[pl.ds(own, share), :] = send_d[pl.ds(own, share), :]
+    recv_d[pl.ds(own + share, 2), :] = send_d[pl.ds(own + share, 2), :]
+
+    @pl.when(keeper)
+    def _():
+        recv_d[pl.ds(own + share + 2, SWEEPS + 1), :] = send_d[pl.ds(own + share + 2, SWEEPS + 1), :]
+
+    split_wait(5 * unit, 8 * unit, k_r, False)
 
     def corners(ref, diag, l):
         top, bottom = ref[l, PAD - 8 : PAD, :], ref[l, PAD + rows : PAD + rows + 8, :]
@@ -531,8 +536,7 @@
             inverse = 1.0 / (1.0 + 4.0 * k)
             side_invert[l, at : at + 8, :] = inverse
             side_coupling[l, at : at + 8, :] = k * inverse
-    for copy in x1:
-        copy.wait_recv()
+    split_wait(5 * unit, 8 * unit, f_r, False)
     for l in range(lev):
         for at in (PAD - 8, PAD + rows):
             k = ka[l, at : at + 8, :]
@@ -545,16 +549,49 @@
 
         sided(adv_send, adv_recv, 8 * l, put)
         corner[0, 8 * l : 8 * l + 8, :], corner[1, 8 * l : 8 * l + 8, :] = corners(field, adv_diag, l)
-
-    for copy in d_copies:
-        copy.wait_recv()
-    for l in range(lev):
-        @pl.when(lon != l * slices + tip_slice)
-        def _(l=l):
-            pltpu.make_async_remote_copy(
-                src_ref=cross_send.at[pl.ds(0, 5), :], dst_ref=cross_recv.at[pl.ds(8 * l, 5), :],
-                send_sem=c_ss.at[0], recv_sem=c_rs.at[l], device_id=(lat, sector(1)), device_id_type=MESH,
-            ).wait_recv()
+        at = 32 * l
+        early[0, l, 12:44, :] = side_tiles[at : at + 32, :]
+        early[0, l, 4:12, :], early[0, l, 44:52, :] = capped(
+            side_tiles[at : at + 8, :], side_tiles[at + 24 : at + 32, :],
+            corner[0, 8 * l : 8 * l + 8, :], corner[1, 8 * l : 8 * l + 8, :],
+        )
+        early_scaled[l, 8:48, :] = early[0, l, 8:48, :] * side_invert[l, 8:48, :]
+
+    weights = shift_weights(width)
+    order = [(0, -1)] + [(i // 4, i % 4) for i in range(groups)] + [(groups // 4 - 1, 4)]
+    at16 = lane & 15
+
+    def sweep_early(t, carry):
+        for l in range(lev):
+            ends = {kk: rim(early[t, l, 12 + 8 * kk : 20 + 8 * kk, :], at16) for kk in range(-1, 5)}
+            total = west_and_east(
+                stack[t, l, PAD - 8 : PAD + rows + 8, :],
+                [jnp.where((lane >> 4) == g, ends[kk], 0.0) for g, kk in order], weights,
+            )
+            for i in range(groups + 2):
+                at = PAD - 8 + 8 * i
+                value = total[8 * i : 8 * i + 8] + (stack[t, l, at - 1 : at + 7, :] + stack[t, l, at + 1 : at + 9, :])
+                stack[t + 1, l, at : at + 8, :] = scaled[l, at : at + 8, :] + coupling[l, at : at + 8, :] * value
+            for j in range(5):
+                at = 8 + 8 * j
+                x = early[t, l, at : at + 8, :]
+                value = roll(x, 1) + roll(x, -1) + early[t, l, at - 1 : at + 7, :] + early[t, l, at + 1 : at + 9, :]
+                early[t + 1, l, at : at + 8, :] = (
+                    early_scaled[l, at : at + 8, :] + side_coupling[l, at : at + 8, :] * value
+                )
+        return carry
+
+    lax.fori_loop(0, SWEEPS, sweep_early, 0)
+
+    plain_rows, more = (share + 2) * (sectors - 1), SWEEPS + 1
+    d_waits = ((keeper, plain_rows + more * (lev - 1)), (jnp.logical_not(keeper), plain_rows + more * lev))
+    for here, count in d_waits:
+        @pl.when(here)
+        def _(count=count):
+            bulk(count, d_r).wait_recv()
+
+    def cross(l, t):
+        return recv_d[pl.ds((l * slices + tip_slice) * DEEP + share + 2 + t, 1), :]
 
     @pl.when(polar)
     def _():
@@ -568,16 +605,16 @@
     @pl.when(north)
     def _():
         for l in range(lev):
-            field[l, PAD - 1 : PAD, :] = cross_recv[8 * l : 8 * l + 1, :]
+            field[l, PAD - 1 : PAD, :] = cross(l, 0)
 
     @pl.when(last)
     def _():
         for l in range(lev):
-            field[l, PAD + rows : PAD + rows + 1, :] = cross_recv[8 * l : 8 * l + 1, :]
-
-    halo = jnp.concatenate([cross_recv[8 * l + 4 : 8 * l + 5, :] for l in range(lev)] * 2, axis=0)
+            field[l, PAD + rows : PAD + rows + 1, :] = cross(l, 0)
+
+    halo = jnp.concatenate([cross(l, SWEEPS) for l in range(lev)] * 2, axis=0)
     for t in range(SWEEPS):
-        plain = jnp.concatenate([cross_recv[8 * l + t : 8 * l + t + 1, :] for l in range(lev)] * 2, axis=0)
+        plain = jnp.concatenate([cross(l, t) for l in range(lev)] * 2, axis=0)
         z = jnp.where(
             lane < 8,
             jnp.where(lane < 4, roll(halo, -8 * t), roll(plain, 4)),
@@ -609,112 +646,94 @@
             at = 8 + 8 * j
             side_scaled[l, at : at + 8, :] = side[l, at : at + 8, :] * side_invert[l, at : at + 8, :]
 
-    for copy in a_copies + x0 + xk + x1 + d_copies:
-        copy.wait_send()
-    for l in range(lev):
-        @pl.when(lon != l * slices + tip_slice)
-        def _(l=l):
-            pole_copy(l).wait_send()
-
-    @pl.when(keeper)
-    def _():
-        for d in range(sectors):
-            @pl.when(lon != d)
-            def _(d=d):
-                cross_copy(d).wait_send()
+    bulk((share + 1) * (sectors - 1), a_s).wait_send()
+    split_wait(3 * unit, 4 * unit, x_s, True)
+    split_wait(5 * unit, 8 * unit, k_s, True)
+    split_wait(5 * unit, 8 * unit, f_s, True)
+    for here, pole_rows, rows_out in (
+        (keeper, 10 * (lev - 1), extra * (sectors - 1)), (jnp.logical_not(keeper), 10 * lev, plain_rows)
+    ):
+        @pl.when(here)
+        def _(pole_rows=pole_rows, rows_out=rows_out):
+            bulk(pole_rows, b_s).wait_send()
+            bulk(rows_out, d_s).wait_send()
 
 
 def relax(
-    bands, field, scaled, coupling, side0, side_scaled, side_coupling, side_cross, filtered, balanced, stack, side, sems
+    bands, stack, scaled, coupling, side0, side_scaled, side_coupling, side_cross, filtered, balanced, local, side, sems
 ):
     lev, rows, width = filtered.shape
-    groups = rows // 8
-    bf16, f32 = jnp.bfloat16, jnp.float32
+    near = local.shape[2] - 2 * PAD
+    tiles = near // 8 + 2
     lat = lax.axis_index("lat")
     north, last = lat == 0, lat == bands - 1
-    out = pltpu.make_async_copy(field.at[:, pl.ds(PAD, rows), :], filtered, sems.at[0])
-    out.start()
+    base = pl.multiple_of(jnp.where(last, rows - near, 0), 8)
+    rest = pl.multiple_of(jnp.where(last, 0, near), 8)
+    copies = [
+        pltpu.make_async_copy(stack.at[0, :, pl.ds(PAD, rows), :], filtered, sems.at[0]),
+        pltpu.make_async_copy(
+            stack.at[SWEEPS, :, pl.ds(rest + PAD, rows - near), :], balanced.at[:, pl.ds(rest, rows - near), :], sems.at[1]
+        ),
+    ]
+    for copy in copies:
+        copy.start()
     lane = lax.broadcasted_iota(jnp.int32, (8, width), 1)
     row8 = lax.broadcasted_iota(jnp.int32, (8, width), 0)
     at16 = lane & 15
-    one = lax.broadcasted_iota(jnp.int32, (width, width), 0)
-    two = lax.broadcasted_iota(jnp.int32, (width, width), 1)
-    shift = jnp.where((one - two == 1) | (two - one == 1), 1.0, 0.0).astype(bf16)
-    spot = one & 15
-    from_west = (two == 0) & ((spot == 3) | (spot == 4))
-    from_east = (two == width - 1) & ((spot == 12) | (spot == 13))
-    weights = jnp.concatenate([shift, shift, jnp.where(from_west | from_east, 1.0, 0.0).astype(bf16)], axis=0)
-
-    def roll(x, by):
-        return pltpu.roll(x, by % width, 1)
-
-    def parts(x):
-        high = x.astype(bf16)
-        return high, (x - high.astype(f32)).astype(bf16)
-
-    def level(source, target, beside, l):
-        ends = {}
-        for kk in range(-1, 5):
-            high, low = parts(beside(l, 12 + 8 * kk))
-            ends[kk] = jnp.where(
-                (at16 == 3) | (at16 == 12), high.astype(f32),
-                jnp.where((at16 == 4) | (at16 == 13), roll(low.astype(f32), 1), 0.0),
-            )
-        order = [(0, -1)] + [(i // 4, i % 4) for i in range(groups)] + [(groups // 4 - 1, 4)]
-        high, low = parts(source(l, PAD - 8, rows + 16))
-        edge = jnp.concatenate([jnp.where((lane >> 4) == g, ends[kk], 0.0) for g, kk in order], axis=0).astype(bf16)
-        total = jnp.dot(jnp.concatenate([high, low, edge], axis=1), weights, preferred_element_type=f32)
-        for i in range(groups + 2):
-            at = PAD - 8 + 8 * i
-            value = total[8 * i : 8 * i + 8] + (source(l, at - 1, 8) + source(l, at + 1, 8))
-            target(l, at, scaled[l, at : at + 8, :] + coupling[l, at : at + 8, :] * value)
-
+    group = (lane >> 4) - jnp.where(last, (rows - near) // 32, 0)
+    weights = shift_weights(width)
     for l in range(lev):
-        stack[0, l, PAD - 16 : PAD + rows + 16, :] = field[l]
-        side[0, l] = side0[l]
-
-    def sweep(t, carry):
-        def source(l, at, count):
-            return stack[t, l, at : at + count, :]
-
-        def target(l, at, value):
-            stack[t + 1, l, at : at + 8, :] = value
-
-        def beside(l, at):
-            return side[t, l, at : at + 8, :]
-
+        local[0, l, PAD - 8 : PAD + near + 8, :] = stack[0, l, pl.ds(base + PAD - 8, near + 16), :]
+    for t in range(SWEEPS):
+        beside = side0 if t == 0 else side.at[t - 1]
+        edges = []
         for l in range(lev):
-            level(source, target, beside, l)
+            ends = {kk: rim(beside[l, 12 + 8 * kk : 20 + 8 * kk, :], at16) for kk in range(-1, 5)}
+            edges.append(jnp.where(lane < 16, ends[-1], 0.0))
+            for i in range(near // 8):
+                edges.append(jnp.where(group == i // 4, ends[i % 4], 0.0))
+            edges.append(jnp.where(lane >= width - 16, ends[4], 0.0))
+        whole = jnp.concatenate([local[t, l, PAD - 8 : PAD + near + 8, :] for l in range(lev)], axis=0)
+        total = west_and_east(whole, edges, weights)
+        for l in range(lev):
+            for i in range(tiles):
+                at = PAD - 8 + 8 * i
+                start = 8 * (tiles * l + i)
+                value = total[start : start + 8] + (local[t, l, at - 1 : at + 7, :] + local[t, l, at + 1 : at + 9, :])
+                there = pl.ds(base + at, 8)
+                value = scaled[l, there, :] + coupling[l, there, :] * value
+                if t < SWEEPS - 1 and i in (0, tiles - 1):
+                    cross = side_cross[t + 1, 8 + l : 9 + l, :]
+                    if i == 0:
+                        at_end = rows - near + PAD - 8
+                        value = jnp.where(north & (row8 == 7), cross, value)
+                        value = jnp.where(last, stack[t + 1, l, at_end : at_end + 8, :], value)
+                    else:
+                        at_end = near + PAD
+                        value = jnp.where(
+                            last, jnp.where(row8 == 0, cross, value), stack[t + 1, l, at_end : at_end + 8, :]
+                        )
+                local[t + 1, l, at : at + 8, :] = value
+        if t == SWEEPS - 1:
+            break
+        for l in range(lev):
             for j in range(5):
                 at = 8 + 8 * j
-                x = beside(l, at)
-                total = roll(x, 1) + roll(x, -1) + beside(l, at - 1) + beside(l, at + 1)
-                x = side_scaled[l, at : at + 8, :] + side_coupling[l, at : at + 8, :] * total
-                cross = side_cross[t + 1, pl.ds(l, 1), :]
+                x = beside[l, at : at + 8, :]
+                value = pltpu.roll(x, 1, 1) + pltpu.roll(x, width - 1, 1)
+                value = value + (beside[l, at - 1 : at + 7, :] + beside[l, at + 1 : at + 9, :])
+                x = side_scaled[l, at : at + 8, :] + side_coupling[l, at : at + 8, :] * value
+                cross = side_cross[t + 1, l : l + 1, :]
                 if j == 0:
                     x = jnp.where(north & (row8 == 3) & (lane < 16), cross, x)
                 if j == 4:
                     x = jnp.where(last & (row8 == 4) & (lane >= width - 16), cross, x)
-                side[t + 1, l, at : at + 8, :] = x
-        for l in range(lev):
-            cross = side_cross[t + 1, pl.ds(8 + l, 1), :]
-            for here, at in ((north, PAD - 1), (last, PAD + rows)):
-                stack[t + 1, l, at : at + 1, :] = jnp.where(here, cross, stack[t + 1, l, at : at + 1, :])
-        return carry
-
-    lax.fori_loop(0, SWEEPS - 1, sweep, 0)
-    copies = [out]
-    for l in range(lev):
-        level(
-            lambda l, at, count: stack[SWEEPS - 1, l, at : at + count, :],
-            lambda l, at, value: stack.__setitem__((SWEEPS, l, slice(at, at + 8), slice(None)), value),
-            lambda l, at: side[SWEEPS - 1, l, at : at + 8, :],
-            l,
-        )
-        copy = pltpu.make_async_copy(stack.at[SWEEPS, l, pl.ds(PAD, rows), :], balanced.at[l], sems.at[1 + l])
-        copy.start()
-        copies.append(copy)
-    for copy in copies:
+                side[t, l, at : at + 8, :] = x
+    copy = pltpu.make_async_copy(
+        local.at[SWEEPS, :, pl.ds(PAD, near), :], balanced.at[:, pl.ds(base, near), :], sems.at[2]
+    )
+    copy.start()
+    for copy in (*copies, copy):
         copy.wait()
 
 
@@ -735,24 +754,27 @@
         narrow = array(lev, 56, width)
         vmem = pl.BlockSpec(memory_space=pltpu.VMEM)
         hbm = pl.BlockSpec(memory_space=pltpu.HBM)
-        small = (cutoff.reshape(1, -1), partner.reshape(sectors, width), *tables(sectors, width))
+        tw_cos, tw_sin, fwd, inv = tables(sectors, width)
+        blank = np.zeros((16 - tw_cos.shape[0], width), np.float32)
+        table = np.concatenate([tw_cos, blank, tw_sin, blank, fwd, inv[:, :width], inv[:, width:]], axis=0)
+        small = (cutoff.reshape(1, -1), partner.reshape(sectors, width), table)
         dma = pltpu.SemaphoreType.DMA
-        made = [(lev, high, width)] * 3 + [(lev, 56, width)] * 3 + [(SWEEPS, 16, width)]
+        made = [(SWEEPS + 1, lev, high, width)] + [(lev, high, width)] * 2 + [(lev, 56, width)] * 3 + [(SWEEPS, 16, width)]
         limit = 24 * 1024 * 1024
+        near = cutoff.shape[0] // 2 + 32
         held = pl.pallas_call(
             functools.partial(kernel, sectors, bands),
             out_shape=[jax.ShapeDtypeStruct(shape, f32) for shape in made],
-            in_specs=[hbm] * 10,
+            in_specs=[hbm] * 7,
             out_specs=[vmem] * len(made),
             scratch_shapes=[
                 tall, block, block, tall,
                 *[pltpu.VMEM(a.shape, a.dtype) for a in small],
-                dma((10,)),
+                dma((7,)),
                 strips, strips, array(16 * lev, width), array(16 * sectors, width), strips, strips,
-                array(8 * sectors, width), array(8 * lev, width), array(sectors, width),
-                pair, pair, pair, pair, four, pair, pair, four, pair, tall, array(lev * 32, width), narrow,
-                *[dma((sectors,))] * 4,
-                dma((lev,)), dma((sectors,)), dma((sectors,)), dma((lev,)), dma((20,)), dma((20,)),
+                array(sectors, width),
+                pair, pair, pair, pair, four, pair, pair, four, pair, tall, array(lev * 32, width), narrow, array(SWEEPS + 1, lev, 56, width), narrow,
+                *[dma] * 12,
             ],
             compiler_params=pltpu.CompilerParams(collective_id=0, has_side_effects=True, vmem_limit_bytes=limit),
         )(
@@ -763,7 +785,7 @@
             out_shape=[jax.ShapeDtypeStruct(tracer.shape, f32)] * 2,
             in_specs=[vmem] * len(made),
             out_specs=[hbm] * 2,
-            scratch_shapes=[array(SWEEPS + 1, lev, high, width), array(SWEEPS, lev, 56, width), dma((1 + lev,))],
+            scratch_shapes=[array(SWEEPS + 1, lev, near + 2 * PAD, width), array(SWEEPS - 1, lev, 56, width), dma((3,))],
             compiler_params=pltpu.CompilerParams(vmem_limit_bytes=limit),
         )(*[pltpu.with_memory_space_constraint(a, pltpu.VMEM) for a in held])
 

time: 24.1 us -> 22.9 us (0.950)
  Pallas kernels: 23.3 us -> 22.1 us
    pallas_call x1, Pallas kernels: 2.79 us -> 1.55 us  [per_device(): pl.pallas_call(functools.partial(relax, bands), out_shape=[jax.ShapeDtype...]
where the time goes in v3:
time: 22.9 us; the launch traced here: 22.8 us
  Pallas kernels  22.1 us (97%)
  between operations  0.64 us (3%)
    pallas_call x1, Pallas kernels, per_device(): pl.pallas_call(functools.partial(kernel, sectors, bands), out_shape=[jax....  20.6 us
    pallas_call x1, Pallas kernels, per_device(): pl.pallas_call(functools.partial(relax, bands), out_shape=[jax.ShapeDtype...  1.55 us

profile of v3, /device:TPU:0, one launch (start us, length us, event | category | flops | bytes accessed | tf_op | source)
XLA Modules:
  0.0 22.8 jit_solution(10377744872013134244)
XLA Ops:
  0.6 20.6 %shard_map.86 = (f32[5,4,288,128]{3,2,1,0:T(8,128)S(1)}, f32[4,288,128]{2,1,0:T(8,128)S(1)}, f32[4,288,128]{2,1,0:T(8,128)S(1)}, f32[4,56,128]{2,1,0:T(8,128)S(1...) custom-call(f32[4,256,128]{2,1,0:T(8,128)} %tracer_h.1, ...), custom_call_target="tpu_custom_call" | custom-call | tf_op jit(solution)/shard_map/pallas_call | solution.py:765
  21.2 1.5 %shard_map.87 = (f32[4,256,128]{2,1,0:T(8,128)}, f32[4,256,128]{2,1,0:T(8,128)}) custom-call(f32[5,4,288,128]{3,2,1,0:T(8,128)S(1)} %get-tuple-element.9.stack, f32[4,288,128]{2,1,0:T(8,128)S(1)} %get-tuple-element.10.scaled, f32[4,288,128]{2,1,0:T(8,128)S(1)} %get-tuple-element.11.coupling, f32[4,56,128]{2,1,0:T(8,128)S(1)} %get-tuple-element.12.side0, ...), custom_call_target="tpu_custom_call" | custom-call | tf_op jit(solution)/shard_map/pallas_call | solution.py:783

commit v4 on v3

--- a/solution.py
+++ b/solution.py
@@ -62,6 +62,14 @@
     from_east = (two == width - 1) & ((spot == 12) | (spot == 13))
     edge = jnp.where(from_west | from_east, 1.0, 0.0).astype(jnp.bfloat16)
     return jnp.concatenate([shift, shift, edge], axis=0)
+
+
+def change_weights(width):
+    one = lax.broadcasted_iota(jnp.int32, (width, width), 0)
+    two = lax.broadcasted_iota(jnp.int32, (width, width), 1)
+    shift = (jnp.where(one - two == 1, 1.0, 0.0) - jnp.where(two - one == 1, 1.0, 0.0)).astype(jnp.bfloat16)
+    edge = jnp.where((two == width - 1) & ((one & 1) == 0), 1.0, 0.0) - jnp.where((two == 0) & ((one & 1) == 1), 1.0, 0.0)
+    return jnp.concatenate([shift, shift, edge.astype(jnp.bfloat16)], axis=0)
 
 
 def rim(h, at16):
@@ -194,8 +202,6 @@
     for h, v in enumerate(swapped(*packs)):
         send_a[pl.ds(8 * h * DEEP + share, 8, stride=DEEP), :] = v
 
-    pl.semaphore_wait(barrier, sectors - 1 + 3 * len(beside))
-
     def across(src, dst, count, ss, rs):
         for t in range(1, sectors):
             there = sector(t)
@@ -219,8 +225,6 @@
                     bulk(count, sem).wait_send()
                 else:
                     bulk(count, sem).wait_recv()
-
-    across(send_a, recv_a, share + 1, a_s, a_r)
 
     four = lane >> 2
 
@@ -270,8 +274,10 @@
 
     unit = 8 * lev
     pack_rims(tr, rim_send)
+    pl.semaphore_wait(barrier, sectors - 1 + 3 * len(beside))
     sideways(rim_send, rim_recv, x_s, x_r)
     poleward(tr, x_s, x_r)
+    across(send_a, recv_a, share + 1, a_s, a_r)
 
     loads[3].wait()
     for l in range(lev):
@@ -313,22 +319,23 @@
             farther, taken(pltpu.roll(points, sectors - half - 1, 0), at_lane), taken(pltpu.roll(points, half, 0), at_lane)
         )
 
+
+    change = change_weights(width)
     split_wait(3 * unit, 4 * unit, x_r, False)
-
-    def renew(l, carry):
-        at = pl.multiple_of(8 * l, 8)
-        rim = jnp.where(
-            (lane & 3) == 3, rim_recv[0, pl.ds(at, 8), :], roll(rim_recv[1, pl.ds(at, 8), :], -2)
+    for l in range(lev):
+        edge = jnp.where((lane & 3) == 3, rim_recv[0, 8 * l : 8 * l + 8, :], roll(rim_recv[1, 8 * l : 8 * l + 8, :], -2))
+        high, low = parts(edge)
+        edge = jnp.where((lane & 3) >= 2, high.astype(jnp.float32), roll(low.astype(jnp.float32), -2))
+        across_east = west_and_east(
+            tr[l, PAD : PAD + rows, :], [jnp.where(four == g, edge, 0.0) for g in range(groups)], change
         )
         tiles = []
         for g in range(groups):
             at = PAD + 8 * g
             x = tr[l, at : at + 8, :]
-            h = roll(rim, -(4 * g + 3))
-            w = jnp.where(lane == 0, h, roll(x, 1))
-            e = jnp.where(lane == width - 1, h, roll(x, -1))
             turn = wn[l, 8 * g : 8 * g + 8, :] * (tr[l, at + 1 : at + 9, :] - tr[l, at - 1 : at + 7, :])
-            value = x - COURANT * 0.5 * (we[l, 8 * g : 8 * g + 8, :] * (e - w) + turn)
+            push = we[l, 8 * g : 8 * g + 8, :] * across_east[8 * g : 8 * g + 8]
+            value = x - COURANT * 0.5 * (push + turn)
             field[l, at : at + 8, :] = value
             k = ka[l, at : at + 8, :]
             inverse = 1.0 / (1.0 + 4.0 * k)
@@ -337,12 +344,8 @@
             scaled[l, at : at + 8, :] = value * inverse
             tiles.append(value)
         first, second = packed(tiles)
-        at = pl.multiple_of(8 * l, 8)
-        adv_send[0, pl.ds(at, 8), :] = first
-        adv_send[1, pl.ds(at, 8), :] = second
-        return carry
-
-    lax.fori_loop(0, lev, renew, 0)
+        adv_send[0, 8 * l : 8 * l + 8, :] = first
+        adv_send[1, 8 * l : 8 * l + 8, :] = second
 
     def sided(send, recv, at, put):
         for kk in range(4):
@@ -394,12 +397,12 @@
     ends = (lane == 0) | (lane == width - 1)
     spread = []
     for d in range(sectors):
-        parts = []
+        halves = []
         for h in range(2):
             x = recv_a[d * DEEP + 8 * h : d * DEEP + 8 * h + 8, :]
             x = x + jnp.where(ends, roll(fixes[h], -(8 * d + 6)), 0.0)
-            parts.append(x + jnp.where(at_tip[h], beyond_fix[d : d + 1, :], 0.0))
-        spread.append(jnp.concatenate(parts, axis=0))
+            halves.append(x + jnp.where(at_tip[h], beyond_fix[d : d + 1, :], 0.0))
+        spread.append(jnp.concatenate(halves, axis=0))
 
     def circle(d, k):
         angle = 2.0 * math.pi * ((d * k) % sectors) / sectors

time: 22.9 us -> 21 us (0.917)
  Pallas kernels: 22.1 us -> 20.2 us
    pallas_call x1, Pallas kernels: 20.6 us -> 18.6 us  [per_device(): pl.pallas_call(functools.partial(kernel, sectors, bands), out_shape=[jax....]
where the time goes in v4:
time: 21 us; the launch traced here: 20.8 us
  Pallas kernels  20.2 us (96%)
  between operations  0.64 us (3%)
    pallas_call x1, Pallas kernels, per_device(): pl.pallas_call(functools.partial(kernel, sectors, bands), out_shape=[jax....  18.6 us
    pallas_call x1, Pallas kernels, per_device(): pl.pallas_call(functools.partial(relax, bands), out_shape=[jax.ShapeDtype...  1.55 us

profile of v4, /device:TPU:0, one launch (start us, length us, event | category | flops | bytes accessed | tf_op | source)
XLA Modules:
  0.0 20.8 jit_solution(7194373784929620240)
XLA Ops:
  0.6 18.6 %shard_map.86 = (f32[5,4,288,128]{3,2,1,0:T(8,128)S(1)}, f32[4,288,128]{2,1,0:T(8,128)S(1)}, f32[4,288,128]{2,1,0:T(8,128)S(1)}, f32[4,56,128]{2,1,0:T(8,128)S(1...) custom-call(f32[4,256,128]{2,1,0:T(8,128)} %tracer_h.1, ...), custom_call_target="tpu_custom_call" | custom-call | tf_op jit(solution)/shard_map/pallas_call | solution.py:768
  19.3 1.5 %shard_map.87 = (f32[4,256,128]{2,1,0:T(8,128)}, f32[4,256,128]{2,1,0:T(8,128)}) custom-call(f32[5,4,288,128]{3,2,1,0:T(8,128)S(1)} %get-tuple-element.9.stack, f32[4,288,128]{2,1,0:T(8,128)S(1)} %get-tuple-element.10.scaled, f32[4,288,128]{2,1,0:T(8,128)S(1)} %get-tuple-element.11.coupling, f32[4,56,128]{2,1,0:T(8,128)S(1)} %get-tuple-element.12.side0, ...), custom_call_target="tpu_custom_call" | custom-call | tf_op jit(solution)/shard_map/pallas_call | solution.py:786

commit v5 on v4

--- a/solution.py
+++ b/solution.py
@@ -53,44 +53,42 @@
     return high, (x - high.astype(jnp.float32)).astype(jnp.bfloat16)
 
 
-def shift_weights(width):
+def shift_weights(width, east, west_lane, east_lane, lanes):
     one = lax.broadcasted_iota(jnp.int32, (width, width), 0)
     two = lax.broadcasted_iota(jnp.int32, (width, width), 1)
-    shift = jnp.where((one - two == 1) | (two - one == 1), 1.0, 0.0).astype(jnp.bfloat16)
-    spot = one & 15
-    from_west = (two == 0) & ((spot == 3) | (spot == 4))
-    from_east = (two == width - 1) & ((spot == 12) | (spot == 13))
-    edge = jnp.where(from_west | from_east, 1.0, 0.0).astype(jnp.bfloat16)
-    return jnp.concatenate([shift, shift, edge], axis=0)
-
-
-def change_weights(width):
-    one = lax.broadcasted_iota(jnp.int32, (width, width), 0)
-    two = lax.broadcasted_iota(jnp.int32, (width, width), 1)
-    shift = (jnp.where(one - two == 1, 1.0, 0.0) - jnp.where(two - one == 1, 1.0, 0.0)).astype(jnp.bfloat16)
-    edge = jnp.where((two == width - 1) & ((one & 1) == 0), 1.0, 0.0) - jnp.where((two == 0) & ((one & 1) == 1), 1.0, 0.0)
-    return jnp.concatenate([shift, shift, edge.astype(jnp.bfloat16)], axis=0)
+    shift = jnp.where(one - two == 1, east, 0.0) + jnp.where(two - one == 1, 1.0, 0.0)
+    spot = one & (lanes - 1)
+    edge = jnp.where((two == width - 1) & (spot == east_lane), east, 0.0)
+    edge = edge + jnp.where((two == 0) & (spot == west_lane), 1.0, 0.0)
+    shift, edge = shift.astype(jnp.bfloat16), edge.astype(jnp.bfloat16)
+    return jnp.concatenate([shift, shift, edge, edge], axis=0)
 
 
 def rim(h, at16):
-    high, low = parts(h)
-    return jnp.where(
-        (at16 == 3) | (at16 == 12), high.astype(jnp.float32),
-        jnp.where((at16 == 4) | (at16 == 13), pltpu.roll(low.astype(jnp.float32), 1, 1), 0.0),
-    )
+    high, low = parts(jnp.where((at16 == 3) | (at16 == 12), h, 0.0))
+    return high.astype(jnp.float32), low.astype(jnp.float32)
+
+
+def masked(here, pair):
+    return [jnp.where(here, x, 0.0) for x in pair]
 
 
 def west_and_east(x, edges, weights):
     high, low = parts(x)
-    rims = jnp.concatenate(edges, axis=0).astype(jnp.bfloat16)
-    return jnp.dot(jnp.concatenate([high, low, rims], axis=1), weights, preferred_element_type=jnp.float32)
+    rims = [jnp.concatenate(tiles, axis=0).astype(jnp.bfloat16) for tiles in zip(*edges)]
+    return jnp.dot(jnp.concatenate([high, low, *rims], axis=1), weights, preferred_element_type=jnp.float32)
+
+
+def refined(x, weights):
+    high, low = parts(x)
+    return jnp.dot(jnp.concatenate([high, low, high], axis=1), weights, preferred_element_type=jnp.float32)
 
 
 def kernel(
     sectors, bands,
-    tracer_h, wind_east_h, wind_north_h, kappa_h, cutoff_h, partner_h, table_h,
+    tracer_h, wind_east_h, wind_north_h, kappa_h, cutoff_h, partner_h, table_h, fine_h,
     stack, scaled, coupling, side, side_scaled, side_coupling, side_cross,
-    tr, we, wn, ka, cutoff, partner, table, load_s,
+    tr, we, wn, ka, cutoff, partner, table, fine, load_s,
     send_a, recv_a, pole_send, pole_recv, send_d, recv_d, beyond_fix,
     rim_send, rim_recv, kap_send, kap_recv, kap_diag, adv_send, adv_recv, adv_diag, corner, invert, side_tiles, side_invert, early, early_scaled,
     a_s, a_r, b_s, b_r, d_s, d_r, x_s, x_r, k_s, k_r, f_s, f_r,
@@ -115,8 +113,8 @@
         return lax.rem(lat + (offset % bands), bands)
 
     body = pl.ds(PAD, rows)
-    held = (tracer_h, wind_east_h, wind_north_h, kappa_h, partner_h, cutoff_h, table_h)
-    near = (tr.at[:, body, :], we, wn, ka.at[:, body, :], partner, cutoff, table)
+    held = (tracer_h, wind_east_h, wind_north_h, kappa_h, partner_h, cutoff_h, table_h, fine_h)
+    near = (tr.at[:, body, :], we, wn, ka.at[:, body, :], partner, cutoff, table, fine)
     loads = [pltpu.make_async_copy(h, v, load_s.at[i]) for i, (h, v) in enumerate(zip(held, near))]
     for load in loads[:3]:
         load.start()
@@ -320,22 +318,21 @@
         )
 
 
-    change = change_weights(width)
+    change = shift_weights(width, -1.0, 3, 2, 4)
     split_wait(3 * unit, 4 * unit, x_r, False)
     for l in range(lev):
         edge = jnp.where((lane & 3) == 3, rim_recv[0, 8 * l : 8 * l + 8, :], roll(rim_recv[1, 8 * l : 8 * l + 8, :], -2))
-        high, low = parts(edge)
-        edge = jnp.where((lane & 3) >= 2, high.astype(jnp.float32), roll(low.astype(jnp.float32), -2))
-        across_east = west_and_east(
-            tr[l, PAD : PAD + rows, :], [jnp.where(four == g, edge, 0.0) for g in range(groups)], change
+        edge = [x.astype(jnp.float32) for x in parts(edge)]
+        across_west = west_and_east(
+            tr[l, PAD : PAD + rows, :], [masked(four == g, edge) for g in range(groups)], change
         )
         tiles = []
         for g in range(groups):
             at = PAD + 8 * g
             x = tr[l, at : at + 8, :]
             turn = wn[l, 8 * g : 8 * g + 8, :] * (tr[l, at + 1 : at + 9, :] - tr[l, at - 1 : at + 7, :])
-            push = we[l, 8 * g : 8 * g + 8, :] * across_east[8 * g : 8 * g + 8]
-            value = x - COURANT * 0.5 * (push + turn)
+            push = we[l, 8 * g : 8 * g + 8, :] * across_west[8 * g : 8 * g + 8]
+            value = x + COURANT * 0.5 * (push - turn)
             field[l, at : at + 8, :] = value
             k = ka[l, at : at + 8, :]
             inverse = 1.0 / (1.0 + 4.0 * k)
@@ -384,8 +381,8 @@
     recv_a[pl.ds(own + share, 1), :] = send_a[pl.ds(own + share, 1), :]
     bulk((share + 1) * (sectors - 1), a_r).wait_recv()
     tw_cos, tw_sin = table[0 : half + 1, :], table[16 : half + 17, :]
-    fwd = table[32 : 32 + 2 * width, :]
-    inv = jnp.concatenate([table[32 + 2 * width : 32 + 3 * width, :], table[32 + 3 * width : 32 + 4 * width, :]], axis=1)
+    fwd = fine[: 6 * width, :]
+    inv = jnp.concatenate([fine[6 * width : 9 * width, :], fine[9 * width :, :]], axis=1)
 
     def rows_of(ref, at):
         return [ref[pl.ds(8 * h * DEEP + at, 8, stride=DEEP), :] for h in range(2)]
@@ -419,15 +416,11 @@
             blocks.append(jnp.concatenate([re * c, -(re * s)], axis=1))
         else:
             blocks.append(jnp.concatenate([re * c + im * s, im * c - re * s], axis=1))
-    spectrum = jnp.dot(
-        jnp.concatenate(blocks, axis=0), fwd, precision=HIGHEST, preferred_element_type=jnp.float32
-    )
+    spectrum = refined(jnp.concatenate(blocks, axis=0), fwd)
     keep = jnp.concatenate(
         [jnp.where(jnp.abs(wave + k).astype(jnp.float32) <= limit, 1.0, 0.0) for k in range(half + 1)], axis=0
     )
-    back = jnp.dot(
-        jnp.where(keep > 0.0, spectrum, 0.0), inv, precision=HIGHEST, preferred_element_type=jnp.float32
-    )
+    back = refined(jnp.where(keep > 0.0, spectrum, 0.0), inv)
     real, imag = [], []
     for k in range(half + 1):
         c, s = tw_cos[k : k + 1, :], tw_sin[k : k + 1, :]
@@ -560,7 +553,7 @@
         )
         early_scaled[l, 8:48, :] = early[0, l, 8:48, :] * side_invert[l, 8:48, :]
 
-    weights = shift_weights(width)
+    weights = shift_weights(width, 1.0, 3, 12, 16)
     order = [(0, -1)] + [(i // 4, i % 4) for i in range(groups)] + [(groups // 4 - 1, 4)]
     at16 = lane & 15
 
@@ -569,7 +562,7 @@
             ends = {kk: rim(early[t, l, 12 + 8 * kk : 20 + 8 * kk, :], at16) for kk in range(-1, 5)}
             total = west_and_east(
                 stack[t, l, PAD - 8 : PAD + rows + 8, :],
-                [jnp.where((lane >> 4) == g, ends[kk], 0.0) for g, kk in order], weights,
+                [masked((lane >> 4) == g, ends[kk]) for g, kk in order], weights,
             )
             for i in range(groups + 2):
                 at = PAD - 8 + 8 * i
@@ -667,7 +660,7 @@
 ):
     lev, rows, width = filtered.shape
     near = local.shape[2] - 2 * PAD
-    tiles = near // 8 + 2
+    tiles = near // 8 + 1
     lat = lax.axis_index("lat")
     north, last = lat == 0, lat == bands - 1
     base = pl.multiple_of(jnp.where(last, rows - near, 0), 8)
@@ -684,19 +677,18 @@
     row8 = lax.broadcasted_iota(jnp.int32, (8, width), 0)
     at16 = lane & 15
     group = (lane >> 4) - jnp.where(last, (rows - near) // 32, 0)
-    weights = shift_weights(width)
+    weights = shift_weights(width, 1.0, 3, 12, 16)
     for l in range(lev):
         local[0, l, PAD - 8 : PAD + near + 8, :] = stack[0, l, pl.ds(base + PAD - 8, near + 16), :]
     for t in range(SWEEPS):
         beside = side0 if t == 0 else side.at[t - 1]
         edges = []
         for l in range(lev):
-            ends = {kk: rim(beside[l, 12 + 8 * kk : 20 + 8 * kk, :], at16) for kk in range(-1, 5)}
-            edges.append(jnp.where(lane < 16, ends[-1], 0.0))
+            ends = {kk: rim(beside[l, 12 + 8 * kk : 20 + 8 * kk, :], at16) for kk in range(-1, 4)}
+            edges.append(masked(lane < 16, ends[-1]))
             for i in range(near // 8):
-                edges.append(jnp.where(group == i // 4, ends[i % 4], 0.0))
-            edges.append(jnp.where(lane >= width - 16, ends[4], 0.0))
-        whole = jnp.concatenate([local[t, l, PAD - 8 : PAD + near + 8, :] for l in range(lev)], axis=0)
+                edges.append(masked(group == i // 4, ends[i % 4]))
+        whole = jnp.concatenate([local[t, l, PAD - 8 : PAD + near, :] for l in range(lev)], axis=0)
         total = west_and_east(whole, edges, weights)
         for l in range(lev):
             for i in range(tiles):
@@ -705,17 +697,15 @@
                 value = total[start : start + 8] + (local[t, l, at - 1 : at + 7, :] + local[t, l, at + 1 : at + 9, :])
                 there = pl.ds(base + at, 8)
                 value = scaled[l, there, :] + coupling[l, there, :] * value
-                if t < SWEEPS - 1 and i in (0, tiles - 1):
+                if t < SWEEPS - 1 and i == 0:
                     cross = side_cross[t + 1, 8 + l : 9 + l, :]
-                    if i == 0:
-                        at_end = rows - near + PAD - 8
-                        value = jnp.where(north & (row8 == 7), cross, value)
-                        value = jnp.where(last, stack[t + 1, l, at_end : at_end + 8, :], value)
-                    else:
-                        at_end = near + PAD
-                        value = jnp.where(
-                            last, jnp.where(row8 == 0, cross, value), stack[t + 1, l, at_end : at_end + 8, :]
-                        )
+                    at_end = rows - near + PAD - 8
+                    value = jnp.where(north & (row8 == 7), cross, value)
+                    value = jnp.where(last, stack[t + 1, l, at_end : at_end + 8, :], value)
+                    at_end = near + PAD
+                    local[t + 1, l, at_end : at_end + 8, :] = jnp.where(
+                        last, jnp.broadcast_to(cross, (8, width)), stack[t + 1, l, at_end : at_end + 8, :]
+                    )
                 local[t + 1, l, at : at + 8, :] = value
         if t == SWEEPS - 1:
             break
@@ -759,8 +749,13 @@
         hbm = pl.BlockSpec(memory_space=pltpu.HBM)
         tw_cos, tw_sin, fwd, inv = tables(sectors, width)
         blank = np.zeros((16 - tw_cos.shape[0], width), np.float32)
-        table = np.concatenate([tw_cos, blank, tw_sin, blank, fwd, inv[:, :width], inv[:, width:]], axis=0)
-        small = (cutoff.reshape(1, -1), partner.reshape(sectors, width), table)
+        table = np.concatenate([tw_cos, blank, tw_sin, blank], axis=0)
+        fine = []
+        for whole in (fwd, inv[:, :width], inv[:, width:]):
+            first = whole.astype(jnp.bfloat16)
+            fine += [first, first, (whole - first.astype(np.float32)).astype(jnp.bfloat16)]
+        fine = np.concatenate(fine, axis=0)
+        small = (cutoff.reshape(1, -1), partner.reshape(sectors, width), table, fine)
         dma = pltpu.SemaphoreType.DMA
         made = [(SWEEPS + 1, lev, high, width)] + [(lev, high, width)] * 2 + [(lev, 56, width)] * 3 + [(SWEEPS, 16, width)]
         limit = 24 * 1024 * 1024
@@ -768,12 +763,12 @@
         held = pl.pallas_call(
             functools.partial(kernel, sectors, bands),
             out_shape=[jax.ShapeDtypeStruct(shape, f32) for shape in made],
-            in_specs=[hbm] * 7,
+            in_specs=[hbm] * 8,
             out_specs=[vmem] * len(made),
             scratch_shapes=[
                 tall, block, block, tall,
                 *[pltpu.VMEM(a.shape, a.dtype) for a in small],
-                dma((7,)),
+                dma((8,)),
                 strips, strips, array(16 * lev, width), array(16 * sectors, width), strips, strips,
                 array(sectors, width),
                 pair, pair, pair, pair, four, pair, pair, four, pair, tall, array(lev * 32, width), narrow, array(SWEEPS + 1, lev, 56, width), narrow,

time: 21 us -> 20.5 us (0.976)
  Pallas kernels: 20.2 us -> 19.7 us
    pallas_call x1, Pallas kernels: 18.6 us -> 18.3 us  [per_device(): pl.pallas_call(functools.partial(kernel, sectors, bands), out_shape=[jax....]
where the time goes in v5:
time: 20.5 us; the launch traced here: 20.3 us
  Pallas kernels  19.7 us (96%)
  between operations  0.64 us (3%)
    pallas_call x1, Pallas kernels, per_device(): pl.pallas_call(functools.partial(kernel, sectors, bands), out_shape=[jax....  18.3 us
    pallas_call x1, Pallas kernels, per_device(): pl.pallas_call(functools.partial(relax, bands), out_shape=[jax.ShapeDtype...  1.38 us

profile of v5, /device:TPU:0, one launch (start us, length us, event | category | flops | bytes accessed | tf_op | source)
XLA Modules:
  0.0 20.3 jit_solution(12378008417817606029)
XLA Ops:
  0.6 18.3 %shard_map.95 = (f32[5,4,288,128]{3,2,1,0:T(8,128)S(1)}, f32[4,288,128]{2,1,0:T(8,128)S(1)}, f32[4,288,128]{2,1,0:T(8,128)S(1)}, f32[4,56,128]{2,1,0:T(8,128)S(1...) custom-call(f32[4,256,128]{2,1,0:T(8,128)} %tracer_h.1, ...), custom_call_target="tpu_custom_call" | custom-call | tf_op jit(solution)/shard_map/pallas_call | solution.py:763
  19.0 1.4 %shard_map.96 = (f32[4,256,128]{2,1,0:T(8,128)}, f32[4,256,128]{2,1,0:T(8,128)}) custom-call(f32[5,4,288,128]{3,2,1,0:T(8,128)S(1)} %get-tuple-element.9.stack, f32[4,288,128]{2,1,0:T(8,128)S(1)} %get-tuple-element.10.scaled, f32[4,288,128]{2,1,0:T(8,128)S(1)} %get-tuple-element.11.coupling, f32[4,56,128]{2,1,0:T(8,128)S(1)} %get-tuple-element.12.side0, ...), custom_call_target="tpu_custom_call" | custom-call | tf_op jit(solution)/shard_map/pallas_call | solution.py:781

commit v6 on v5

--- a/solution.py
+++ b/solution.py
@@ -405,17 +405,33 @@
         angle = 2.0 * math.pi * ((d * k) % sectors) / sectors
         return math.cos(angle), math.sin(angle)
 
+    def folded(x, lowest):
+        middle = half // 2
+        pairs = range(lowest, middle)
+        return (
+            {d: x[d] + x[half - d] for d in pairs} | {middle: x[middle]},
+            {d: x[d] - x[half - d] for d in pairs},
+        )
+
+    def cosine_sums(x):
+        plus, minus = folded(x, 0)
+        return [weighted([(circle(d, k)[0], v) for d, v in (minus if k % 2 else plus).items()]) for k in range(half + 1)]
+
+    def sine_sums(x):
+        plus, minus = folded(x, 1)
+        return [None] + [
+            weighted([(circle(d, k)[1], v) for d, v in (plus if k % 2 else minus).items()]) for k in range(1, half)
+        ] + [None]
+
     even = [spread[0]] + [spread[d] + spread[sectors - d] for d in range(1, half)] + [spread[half]]
     odd = [None] + [spread[d] - spread[sectors - d] for d in range(1, half)]
     blocks = []
-    for k in range(half + 1):
+    for k, (re, im) in enumerate(zip(cosine_sums(even), sine_sums(odd))):
         c, s = tw_cos[k : k + 1, :], tw_sin[k : k + 1, :]
-        re = weighted([(circle(d, k)[0], even[d]) for d in range(half + 1)])
-        im = weighted([(-circle(d, k)[1], odd[d]) for d in range(1, half)])
         if im is None:
             blocks.append(jnp.concatenate([re * c, -(re * s)], axis=1))
         else:
-            blocks.append(jnp.concatenate([re * c + im * s, im * c - re * s], axis=1))
+            blocks.append(jnp.concatenate([re * c - im * s, -(im * c) - re * s], axis=1))
     spectrum = refined(jnp.concatenate(blocks, axis=0), fwd)
     keep = jnp.concatenate(
         [jnp.where(jnp.abs(wave + k).astype(jnp.float32) <= limit, 1.0, 0.0) for k in range(half + 1)], axis=0
@@ -430,9 +446,7 @@
         real.append((zr * c - zi * s) * twice)
         imag.append((zr * s + zi * c) * twice)
     smooth = [None] * sectors
-    for d in range(half + 1):
-        p = weighted([(circle(d, k)[0], real[k]) for k in range(half + 1)])
-        q = weighted([(circle(d, k)[1], imag[k]) for k in range(1, half)])
+    for d, (p, q) in enumerate(zip(cosine_sums(real), sine_sums(imag))):
         if q is None:
             smooth[d] = p
         else:
@@ -580,6 +594,15 @@
     lax.fori_loop(0, SWEEPS, sweep_early, 0)
 
     plain_rows, more = (share + 2) * (sectors - 1), SWEEPS + 1
+    bulk((share + 1) * (sectors - 1), a_s).wait_send()
+    split_wait(3 * unit, 4 * unit, x_s, True)
+    split_wait(5 * unit, 8 * unit, k_s, True)
+    split_wait(5 * unit, 8 * unit, f_s, True)
+    for here, pole_rows in ((keeper, 10 * (lev - 1)), (jnp.logical_not(keeper), 10 * lev)):
+        @pl.when(here)
+        def _(pole_rows=pole_rows):
+            bulk(pole_rows, b_s).wait_send()
+
     d_waits = ((keeper, plain_rows + more * (lev - 1)), (jnp.logical_not(keeper), plain_rows + more * lev))
     for here, count in d_waits:
         @pl.when(here)
@@ -589,24 +612,15 @@
     def cross(l, t):
         return recv_d[pl.ds((l * slices + tip_slice) * DEEP + share + 2 + t, 1), :]
 
-    @pl.when(polar)
-    def _():
-        for k in range(sectors):
-            l, q = k // slices, k % slices
-            x = recv_d[k * DEEP : k * DEEP + share, :]
-            at = base + PAD + q * share
-            field[l, pl.ds(at, share), :] = x
-            scaled[l, pl.ds(at, share), :] = x * invert[l, pl.ds(at, share), :]
-
-    @pl.when(north)
-    def _():
-        for l in range(lev):
-            field[l, PAD - 1 : PAD, :] = cross(l, 0)
-
-    @pl.when(last)
-    def _():
-        for l in range(lev):
-            field[l, PAD + rows : PAD + rows + 1, :] = cross(l, 0)
+    for k in range(sectors):
+        l, q = k // slices, k % slices
+        at = pl.ds(base + PAD + q * share, share)
+        x = jnp.where(polar, recv_d[k * DEEP : k * DEEP + share, :], field[l, at, :])
+        field[l, at, :] = x
+        scaled[l, at, :] = x * invert[l, at, :]
+    for l in range(lev):
+        for here, at in ((north, PAD - 1), (last, PAD + rows)):
+            field[l, at : at + 1, :] = jnp.where(here, cross(l, 0), field[l, at : at + 1, :])
 
     halo = jnp.concatenate([cross(l, SWEEPS) for l in range(lev)] * 2, axis=0)
     for t in range(SWEEPS):
@@ -642,16 +656,9 @@
             at = 8 + 8 * j
             side_scaled[l, at : at + 8, :] = side[l, at : at + 8, :] * side_invert[l, at : at + 8, :]
 
-    bulk((share + 1) * (sectors - 1), a_s).wait_send()
-    split_wait(3 * unit, 4 * unit, x_s, True)
-    split_wait(5 * unit, 8 * unit, k_s, True)
-    split_wait(5 * unit, 8 * unit, f_s, True)
-    for here, pole_rows, rows_out in (
-        (keeper, 10 * (lev - 1), extra * (sectors - 1)), (jnp.logical_not(keeper), 10 * lev, plain_rows)
-    ):
+    for here, rows_out in ((keeper, extra * (sectors - 1)), (jnp.logical_not(keeper), plain_rows)):
         @pl.when(here)
-        def _(pole_rows=pole_rows, rows_out=rows_out):
-            bulk(pole_rows, b_s).wait_send()
+        def _(rows_out=rows_out):
             bulk(rows_out, d_s).wait_send()
 
 

time: 20.5 us -> 20.4 us (level)
  no operation moved by 1% of the time
where the time goes in v6:
time: 20.4 us; the launch traced here: 20.3 us
  Pallas kernels  19.7 us (97%)
  between operations  0.64 us (3%)
    pallas_call x1, Pallas kernels, per_device(): pl.pallas_call(functools.partial(kernel, sectors, bands), out_shape=[jax....  18.3 us
    pallas_call x1, Pallas kernels, per_device(): pl.pallas_call(functools.partial(relax, bands), out_shape=[jax.ShapeDtype...  1.38 us

profile of v6, /device:TPU:0, one launch (start us, length us, event | category | flops | bytes accessed | tf_op | source)
XLA Modules:
  0.0 20.3 jit_solution(4052957628525708942)
XLA Ops:
  0.6 18.3 %shard_map.95 = (f32[5,4,288,128]{3,2,1,0:T(8,128)S(1)}, f32[4,288,128]{2,1,0:T(8,128)S(1)}, f32[4,288,128]{2,1,0:T(8,128)S(1)}, f32[4,56,128]{2,1,0:T(8,128)S(1...) custom-call(f32[4,256,128]{2,1,0:T(8,128)} %tracer_h.1, ...), custom_call_target="tpu_custom_call" | custom-call | tf_op jit(solution)/shard_map/pallas_call | solution.py:770
  18.9 1.4 %shard_map.96 = (f32[4,256,128]{2,1,0:T(8,128)}, f32[4,256,128]{2,1,0:T(8,128)}) custom-call(f32[5,4,288,128]{3,2,1,0:T(8,128)S(1)} %get-tuple-element.9.stack, f32[4,288,128]{2,1,0:T(8,128)S(1)} %get-tuple-element.10.scaled, f32[4,288,128]{2,1,0:T(8,128)S(1)} %get-tuple-element.11.coupling, f32[4,56,128]{2,1,0:T(8,128)S(1)} %get-tuple-element.12.side0, ...), custom_call_target="tpu_custom_call" | custom-call | tf_op jit(solution)/shard_map/pallas_call | solution.py:788

commit v7 on v5

--- a/solution.py
+++ b/solution.py
@@ -742,7 +742,7 @@
             return pltpu.VMEM(shape, f32)
 
         block, tall = array(lev, rows, width), array(lev, high, width)
-        strips = array(sectors * DEEP, width)
+        strips = array((sectors + 1) * DEEP, width)
         pair, four = array(2, lev * 8, width), array(4, lev * 8, width)
         narrow = array(lev, 56, width)
         vmem = pl.BlockSpec(memory_space=pltpu.VMEM)

time: 20.5 us -> 20.5 us (level)
  no operation moved by 1% of the time
where the time goes in v7:
time: 20.5 us; the launch traced here: 20.3 us
  Pallas kernels  19.7 us (96%)
  between operations  0.64 us (3%)
    pallas_call x1, Pallas kernels, per_device(): pl.pallas_call(functools.partial(kernel, sectors, bands), out_shape=[jax....  18.3 us
    pallas_call x1, Pallas kernels, per_device(): pl.pallas_call(functools.partial(relax, bands), out_shape=[jax.ShapeDtype...  1.38 us

profile of v7, /device:TPU:0, one launch (start us, length us, event | category | flops | bytes accessed | tf_op | source)
XLA Modules:
  0.0 20.3 jit_solution(12204912835391882708)
XLA Ops:
  0.6 18.3 %shard_map.95 = (f32[5,4,288,128]{3,2,1,0:T(8,128)S(1)}, f32[4,288,128]{2,1,0:T(8,128)S(1)}, f32[4,288,128]{2,1,0:T(8,128)S(1)}, f32[4,56,128]{2,1,0:T(8,128)S(1...) custom-call(f32[4,256,128]{2,1,0:T(8,128)} %tracer_h.1, ...), custom_call_target="tpu_custom_call" | custom-call | tf_op jit(solution)/shard_map/pallas_call | solution.py:763
  19.0 1.4 %shard_map.96 = (f32[4,256,128]{2,1,0:T(8,128)}, f32[4,256,128]{2,1,0:T(8,128)}) custom-call(f32[5,4,288,128]{3,2,1,0:T(8,128)S(1)} %get-tuple-element.9.stack, f32[4,288,128]{2,1,0:T(8,128)S(1)} %get-tuple-element.10.scaled, f32[4,288,128]{2,1,0:T(8,128)S(1)} %get-tuple-element.11.coupling, f32[4,56,128]{2,1,0:T(8,128)S(1)} %get-tuple-element.12.side0, ...), custom_call_target="tpu_custom_call" | custom-call | tf_op jit(solution)/shard_map/pallas_call | solution.py:781

commit v8 on v5

--- a/solution.py
+++ b/solution.py
@@ -116,9 +116,6 @@
     held = (tracer_h, wind_east_h, wind_north_h, kappa_h, partner_h, cutoff_h, table_h, fine_h)
     near = (tr.at[:, body, :], we, wn, ka.at[:, body, :], partner, cutoff, table, fine)
     loads = [pltpu.make_async_copy(h, v, load_s.at[i]) for i, (h, v) in enumerate(zip(held, near))]
-    for load in loads[:3]:
-        load.start()
-
     barrier = pltpu.get_barrier_semaphore()
     for t in range(1, sectors):
         pl.semaphore_signal(barrier, inc=1, device_id=(lat, sector(t)), device_id_type=MESH)
@@ -127,7 +124,7 @@
         for i in (-1, 0, 1):
             pl.semaphore_signal(barrier, inc=1, device_id=(band(t), sector(i)), device_id_type=MESH)
 
-    for load in loads[3:]:
+    for load in loads:
         load.start()
 
     lane = lax.broadcasted_iota(jnp.int32, (8, width), 1)

time: 20.5 us -> 20.5 us (level)
  no operation moved by 1% of the time
where the time goes in v8:
time: 20.5 us; the launch traced here: 20.3 us
  Pallas kernels  19.7 us (96%)
  between operations  0.64 us (3%)
    pallas_call x1, Pallas kernels, per_device(): pl.pallas_call(functools.partial(kernel, sectors, bands), out_shape=[jax....  18.3 us
    pallas_call x1, Pallas kernels, per_device(): pl.pallas_call(functools.partial(relax, bands), out_shape=[jax.ShapeDtype...  1.38 us

profile of v8, /device:TPU:0, one launch (start us, length us, event | category | flops | bytes accessed | tf_op | source)
XLA Modules:
  0.0 20.3 jit_solution(15814163015629846705)
XLA Ops:
  0.6 18.3 %shard_map.95 = (f32[5,4,288,128]{3,2,1,0:T(8,128)S(1)}, f32[4,288,128]{2,1,0:T(8,128)S(1)}, f32[4,288,128]{2,1,0:T(8,128)S(1)}, f32[4,56,128]{2,1,0:T(8,128)S(1...) custom-call(f32[4,256,128]{2,1,0:T(8,128)} %tracer_h.1, ...), custom_call_target="tpu_custom_call" | custom-call | tf_op jit(solution)/shard_map/pallas_call | solution.py:760
  19.0 1.4 %shard_map.96 = (f32[4,256,128]{2,1,0:T(8,128)}, f32[4,256,128]{2,1,0:T(8,128)}) custom-call(f32[5,4,288,128]{3,2,1,0:T(8,128)S(1)} %get-tuple-element.9.stack, f32[4,288,128]{2,1,0:T(8,128)S(1)} %get-tuple-element.10.scaled, f32[4,288,128]{2,1,0:T(8,128)S(1)} %get-tuple-element.11.coupling, f32[4,56,128]{2,1,0:T(8,128)S(1)} %get-tuple-element.12.side0, ...), custom_call_target="tpu_custom_call" | custom-call | tf_op jit(solution)/shard_map/pallas_call | solution.py:778
